TPU v7x, 128 devices: a whole 4x4x4 slice. The times are simulated.
128 devices in a mesh: row: 8 (over z_hi, y), col: 16 (over x, z_lo, core).
Axes of the slice: x: 4, y: 4, z: 4 (z_hi: 2, z_lo: 2; z = z_hi * 2 + z_lo), core: 2. Of those that a mesh axis runs over, the one named last changes fastest.
Arguments:
- cooc: int32 [16384, 32768], P('row', 'col'), may hold values from 0 to 48
- tile_list: int32 [8, 16, 4], P('row', 'col'), may hold values from -1 to 3, as said below
- marginal: int32 [32768], P(('col', 'row')), may hold values from 8 to 524287
- embed: float32 [32768, 256], P(('col', 'row')), may hold values from -1.5 to 1.5
- accum: float32 [32768, 256], P(('col', 'row')), may hold values from 0.001 to 0.01
Outputs:
- new_embed: float32 [32768, 256], P(('col', 'row'))
- new_accum: float32 [32768, 256], P(('col', 'row'))
Inputs may be any that keep to these rules, and one draw needn't show every extreme that they name: `tile_list`: the first entries of each device's list are distinct local tile numbers, the rest are -1; every device lists at least one tile and some device lists all 4.
All inputs are finite; a program needn't handle non-finite values.
Results may differ from a plain program's by a relative error of at most 0.0003.
Values sent between devices are 32-bit elements; how exact they have to be, the bound alone decides.
A program may use at most 128 MiB of HBM per device.

v0:
```python
import jax
import jax.numpy as jnp
from jax import lax
from jax.sharding import PartitionSpec as P

BLOCK = 1024
CB = 2


LEARN_RATE = 0.05


def broadcast(array, axis, root):
    mine = lax.axis_index(axis) == root
    return lax.psum(jnp.where(mine, array, jnp.zeros_like(array)), axis)


def tile_grads(counts, row_vecs, col_vecs, row_logs, col_logs, log_total):
    scores = lax.dot_general(
        row_vecs,
        col_vecs,
        (((1,), (1,)), ((), ())),
        precision=lax.Precision.HIGHEST,
        preferred_element_type=jnp.float32,
    )
    centred = scores + row_logs[:, None] + col_logs[None, :] - log_total
    counts_f = counts.astype(jnp.float32)
    weights = 0.1 + 0.25 * jnp.sqrt(counts_f)
    slopes = jnp.where(
        counts > 0,
        weights * (centred - jnp.log(jnp.maximum(counts_f, 1.0))),
        jax.nn.sigmoid(centred),
    )
    to_rows = jnp.dot(
        slopes, col_vecs, precision=lax.Precision.HIGHEST, preferred_element_type=jnp.float32
    )
    to_cols = lax.dot_general(
        slopes,
        row_vecs,
        (((0,), (0,)), ((), ())),
        precision=lax.Precision.HIGHEST,
        preferred_element_type=jnp.float32,
    )
    return (to_rows, to_cols)


def local(cooc, tile_list, marginal, embed, accum):
    count_total = lax.psum(jnp.sum(marginal.astype(jnp.float32)), ("row", "col"))
    log_total = jnp.log(count_total)
    col_embed, col_marg = (
        lax.all_gather(embed, "row", axis=0, tiled=True),
        lax.all_gather(marginal, "row", axis=0, tiled=True),
    )
    row_index = lax.axis_index("row")
    col_index = lax.axis_index("col")
    row_embed, row_marg = (
        broadcast(col_embed, "col", row_index),
        broadcast(col_marg, "col", row_index),
    )
    row_logs_all = jnp.log(row_marg.astype(jnp.float32))
    col_logs_all = jnp.log(col_marg.astype(jnp.float32))
    listing = tile_list.reshape(-1)
    partials = (jnp.zeros(row_embed.shape, jnp.float32), jnp.zeros(col_embed.shape, jnp.float32))
    for position in range(listing.shape[0]):
        entry = listing[position]
        tile_local = jnp.maximum(entry, 0)
        weight_on = (entry >= 0).astype(jnp.float32)
        add_row_part, add_col_part = partials
        row_start = tile_local // CB * BLOCK
        col_start = tile_local % CB * BLOCK
        counts = lax.dynamic_slice(cooc, (row_start, col_start), (BLOCK, BLOCK))
        row_vecs = lax.dynamic_slice_in_dim(row_embed, row_start, BLOCK, 0)
        col_vecs = lax.dynamic_slice_in_dim(col_embed, col_start, BLOCK, 0)
        row_logs = lax.dynamic_slice_in_dim(row_logs_all, row_start, BLOCK, 0)
        col_logs = lax.dynamic_slice_in_dim(col_logs_all, col_start, BLOCK, 0)
        to_rows, to_cols = tile_grads(counts, row_vecs, col_vecs, row_logs, col_logs, log_total)
        add_row_part = lax.dynamic_update_slice_in_dim(
            add_row_part,
            lax.dynamic_slice_in_dim(add_row_part, row_start, BLOCK, 0) + weight_on * to_rows,
            row_start,
            0,
        )
        add_col_part = lax.dynamic_update_slice_in_dim(
            add_col_part,
            lax.dynamic_slice_in_dim(add_col_part, col_start, BLOCK, 0) + weight_on * to_cols,
            col_start,
            0,
        )
        partials = (add_row_part, add_col_part)
    row_part, col_part = partials
    row_sums = lax.psum(row_part, "col")
    owned = lax.psum_scatter(col_part, "row", scatter_dimension=0, tiled=True)
    groups = lax.axis_size("row")
    root_row = jnp.minimum(col_index, groups - 1)
    relayed = broadcast(row_sums, "row", root_row)
    share_rows = embed.shape[0]
    picked = lax.dynamic_slice_in_dim(relayed, row_index * share_rows, share_rows, 0)
    owned = owned + (col_index < groups).astype(jnp.float32) * picked
    gradients = owned / BLOCK
    new_accum = accum + gradients * gradients
    new_embed = embed - LEARN_RATE * gradients / jnp.sqrt(new_accum)
    return (new_embed, new_accum)


def solution(mesh):
    placed = (
        P("row", "col"),
        P("row", "col", None),
        P(("col", "row")),
        P(("col", "row"), None),
        P(("col", "row"), None),
    )
    return jax.shard_map(
        local,
        mesh=mesh,
        in_specs=placed,
        out_specs=(P(("col", "row"), None), P(("col", "row"), None)),
        check_vma=False,
    )
```

profile of v0, /device:TPU:0, one launch (start us, length us, event | category | flops | bytes accessed | tf_op | source)
XLA Modules:
  0.0 548.6 jit_solution(13451872200994405766)
XLA Ops:
  8.0 59.9 %all-gather.3.cloned.1.call-done = f32[2048,256]{1,0:T(8,128)} async-done(((f32[256,256]{1,0:T(8,128)}), f32[2048,256]{1,0:T(8,128)}) %all-gather.3.cloned.1.call-update) | async-done | bytes 2097168 | tf_op jit(solution)/shard_map/all_gather | solution.py:51
  67.9 3.2 broadcast_select_fusion.1
  71.8 63.3 %psum.37 = f32[]{:T(128)} all-reduce(f32[]{:T(128)} %convert_reduce_fusion), channel_id=1, replica_groups=mesh['row'=8,'col'=16] {'row','col'}, use_global_device_ids=true, to_apply=%region_3.4 | all-reduce | flops 1 | bytes 8 | tf_op jit(solution)/shard_map/psum | solution.py:48
  141.7 19.2 %all-gather = s32[8,1,256]{2,1,0:T(1,128)S(1)} all-gather(s32[1,1,256]{2,1,0:T(1,128)S(1)} %bitcast.32), channel_id=1, replica_groups=mesh['row'=8,'col'=16] {'row'}, dimensions={0}, use_global_device_ids=true | all-gather | bytes 9216 | tf_op jit(solution)/shard_map/all_gather | solution.py:52
  160.9 11.1 %psum.36 = s32[2048]{0:T(1024)S(1)} all-reduce(s32[2048]{0:T(1024)S(1)} %bitcast.31), channel_id=1, replica_groups=mesh['row'=8,'col'=16] {'col'}, use_global_device_ids=true, to_apply=%region_1.0 | all-reduce | flops 2048 | bytes 16384 | tf_op jit(solution)/shard_map/psum | solution.py:15
  172.1 21.0 %all-reduce.4.cloned.1.call-done = f32[2048,256]{1,0:T(8,128)} async-done(((f32[2048,256]{1,0:T(8,128)}), f32[2048,256]{1,0:T(8,128)}) %all-reduce.4.cloned.1.call-update) | async-done | bytes 2097168 | tf_op jit(solution)/shard_map/psum | solution.py:15
  193.2 9.5 %divide_select_fusion.3 = f32[1024,1024]{1,0:T(8,128)S(1)} fusion(s32[2048,2048]{1,0:T(8,128)} %param.5, s32[]{:T(128)S(6)} %select_n.125, s32[]{:T(128)S(6)} %select_n.127, f32[]{:T(128)S(6)} %log.23, f32[1024]{0:T(1024)S(1)} %get-tuple-element.11, f32[1024]{0:T(1024)S(1)} %get-tuple-element.7, f32[2048,256]{1,0:T(8,128)S(1)} %copy-done.2, ...), kind=kOutput, calls=%fused_computation.3 | convolution fusion | flops 3235905536 | bytes 10496512 | tf_op jit(solution)/shard_map/dot_general | solution.py:19
  202.7 10.4 %divide_select_fusion.2 = f32[1024,1024]{1,0:T(8,128)S(1)} fusion(s32[2048,2048]{1,0:T(8,128)} %param.5, s32[]{:T(128)S(6)} %select_n.136, s32[]{:T(128)S(6)} %select_n.134, f32[1024]{0:T(1024)S(1)} %get-tuple-element.10, f32[1024]{0:T(1024)S(1)} %get-tuple-element.6, f32[]{:T(128)S(6)} %log.23, f32[2048,256]{1,0:T(8,128)S(1)} %copy-done.2, ...), kind=kOutput, calls=%fused_computation.2 | convolution fusion | flops 3235905536 | bytes 10496512 | tf_op jit(solution)/shard_map/dot_general | solution.py:19
  213.1 6.8 %divide_select_fusion.1 = f32[1024,1024]{1,0:T(8,128)S(1)} fusion(s32[2048,2048]{1,0:T(8,128)S(1)} %bitcast.34, s32[]{:T(128)S(6)} %select_n.141, s32[]{:T(128)S(6)} %select_n.139, f32[1024]{0:T(1024)S(1)} %get-tuple-element.9, f32[1024]{0:T(1024)S(1)} %get-tuple-element.5, f32[]{:T(128)S(6)} %log.23, f32[2048,256]{1,0:T(8,128)S(1)} %copy-done.2, ...), kind=kOutput, calls=%fused_computation.1 | convolution fusion | flops 3235905536 | bytes 10496512 | tf_op jit(solution)/shard_map/dot_general | solution.py:19
  220.0 7.0 %divide_select_fusion = f32[1024,1024]{1,0:T(8,128)S(1)} fusion(s32[2048,2048]{1,0:T(8,128)S(1)} %bitcast.34, s32[]{:T(128)S(6)} %select_n.146, s32[]{:T(128)S(6)} %select_n.144, f32[1024]{0:T(1024)S(1)} %get-tuple-element.8, f32[1024]{0:T(1024)S(1)} %get-tuple-element.4, f32[]{:T(128)S(6)} %log.23, f32[2048,256]{1,0:T(8,128)S(1)} %copy-done.2, ...), kind=kOutput, calls=%fused_computation | convolution fusion | flops 3235905536 | bytes 10496512 | tf_op jit(solution)/shard_map/dot_general | solution.py:19
  227.1 3.4 fusion.6
  230.6 3.4 fusion.5
  234.0 3.7 fusion.3
  237.7 3.4 fusion.1
  241.1 1.3 copy-done.1
  242.7 9.3 %fusion.13 = f32[2048,256]{1,0:T(8,128)S(1)} fusion(f32[2048,256]{1,0:T(8,128)S(1)} %broadcast.33.clone, s32[]{:T(128)S(6)} %select_n.127, f32[1024,1024]{1,0:T(8,128)} %copy-done.10, f32[2048,256]{1,0:T(8,128)} %all-reduce.4.cloned.1.call-done, s32[]{:T(128)S(6)} %select_n.125, f32[]{:T(128)} %bitcast), kind=kOutput, calls=%fused_computation.25 | convolution fusion | flops 3221487616 | bytes 6291976 | tf_op jit(solution)/shard_map/dot_general | solution.py:37
  252.1 6.9 %fusion.12 = f32[2048,256]{1,0:T(8,128)S(1)} fusion(f32[2048,256]{1,0:T(8,128)S(1)} %fusion.13, s32[]{:T(128)S(6)} %select_n.134, f32[1024,1024]{1,0:T(8,128)S(1)} %copy-done.9, f32[2048,256]{1,0:T(8,128)S(1)} %copy-done.12, s32[]{:T(128)S(6)} %select_n.136, f32[]{:T(128)} %bitcast.8), kind=kOutput, calls=%fused_computation.23 | convolution fusion | flops 3221749760 | bytes 7340044 | tf_op jit(solution)/shard_map/dot_general | solution.py:37
  259.0 7.1 %fusion.10 = f32[2048,256]{1,0:T(8,128)S(1)} fusion(f32[2048,256]{1,0:T(8,128)S(1)} %fusion.12, s32[]{:T(128)S(6)} %select_n.139, f32[1024,1024]{1,0:T(8,128)S(1)} %copy-done.7, f32[2048,256]{1,0:T(8,128)S(1)} %copy-done.12, s32[]{:T(128)S(6)} %select_n.141, f32[]{:T(128)} %bitcast.12), kind=kOutput, calls=%fused_computation.20 | convolution fusion | flops 3221749760 | bytes 7340044 | tf_op jit(solution)/shard_map/dot_general | solution.py:37
  266.2 6.9 %fusion.8 = f32[2048,256]{1,0:T(8,128)S(1)} fusion(f32[2048,256]{1,0:T(8,128)S(1)} %fusion.10, s32[]{:T(128)S(6)} %select_n.144, f32[1024,1024]{1,0:T(8,128)S(1)} %copy-done.5, f32[2048,256]{1,0:T(8,128)S(1)} %copy-done.12, s32[]{:T(128)S(6)} %select_n.146, f32[]{:T(128)} %bitcast.16), kind=kOutput, calls=%fused_computation.17 | convolution fusion | flops 3221749760 | bytes 7340044 | tf_op jit(solution)/shard_map/dot_general | solution.py:37
  274.5 92.1 %all-reduce.6.cloned.1.call-done = f32[2048,256]{1,0:T(8,128)} async-done(((f32[2048,256]{1,0:T(8,128)}), f32[2048,256]{1,0:T(8,128)}) %all-reduce.6.cloned.1.call-update) | async-done | bytes 2097168 | tf_op jit(solution)/shard_map/psum | solution.py:91
  366.6 3.1 broadcast_select_fusion
  369.7 76.6 %reduce-scatter.2.cloned.1.call-done = f32[256,256]{1,0:T(8,128)} async-done(((f32[2048,256]{1,0:T(8,128)}), f32[256,256]{1,0:T(8,128)}) %reduce-scatter.2.cloned.1.call-update) | async-done | bytes 262160 | tf_op jit(solution)/shard_map/reduce_scatter | solution.py:92
  446.4 93.7 %all-reduce.8.cloned.1.call-done = f32[2048,256]{1,0:T(8,128)} async-done(((f32[2048,256]{1,0:T(8,128)}), f32[2048,256]{1,0:T(8,128)}) %all-reduce.8.cloned.1.call-update) | async-done | bytes 2097168 | tf_op jit(solution)/shard_map/psum | solution.py:15
  540.0 1.9 multiply_subtract_fusion
  (61 shorter events, 3.9 us)
Async XLA Ops:
  7.2 64.0 %copy-start.16 = (s32[256]{0:T(256)S(1)}, s32[256]{0:T(256)}, u32[]{:S(2)}) copy-start(s32[256]{0:T(256)} %param.7) | copy-start | bytes 3076
  7.2 127.9 %copy-start.15 = (s32[1,1,4]{2,1,0:T(1,128)S(1)}, s32[1,1,4]{2,1,0:T(1,128)}, u32[]{:S(2)}) copy-start(s32[1,1,4]{2,1,0:T(1,128)} %param.6) | copy-start | bytes 52
  7.2 60.7 %all-gather.3.cloned.1.call-start = ((), (), s32[]{:S(2)}) async-start(), calls=%async_computation.1 | async-start | bytes 2359296 | tf_op jit(solution)/shard_map/all_gather | solution.py:51
  7.9 185.2 %all-reduce.4.cloned.1.call-start = ((), (), s32[]{:S(2)}) async-start(), calls=%async_computation.2 | async-start | bytes 4194304 | tf_op jit(solution)/shard_map/psum | solution.py:15
  67.9 125.3 %copy-start.2 = (f32[2048,256]{1,0:T(8,128)S(1)}, f32[2048,256]{1,0:T(8,128)}, u32[]{:S(2)}) copy-start(f32[2048,256]{1,0:T(8,128)} %all-gather.3.cloned.1.call-done) | copy-start | bytes 6291460
  71.1 295.5 %all-reduce.6.cloned.1.call-start = ((), (), s32[]{:S(2)}) async-start(), calls=%async_computation.4 | async-start | bytes 4194304 | tf_op jit(solution)/shard_map/psum | solution.py:91
  193.2 9.5 %copy-start.11 = (f32[2048,256]{1,0:T(8,128)S(1)}, f32[2048,256]{1,0:T(8,128)}, u32[]{:S(2)}) copy-start(f32[2048,256]{1,0:T(8,128)} %all-reduce.4.cloned.1.call-done) | copy-start | bytes 6291460
  193.2 19.9 %slice-start = ((s8[16777216]{0:T(1024)(128)(4,1)}), s8[4194304]{0:T(1024)(128)(4,1)S(1)}, s32[]{:S(2)}) async-start(s8[16777216]{0:T(1024)(128)(4,1)} %bitcast.33), calls=%async_computation.6 | async-start | bytes 8388608
  193.2 19.9 %slice-start.1 = ((s8[16777216]{0:T(1024)(128)(4,1)}), s8[4194304]{0:T(1024)(128)(4,1)S(1)}, s32[]{:S(2)}) async-start(s8[16777216]{0:T(1024)(128)(4,1)} %bitcast.33), calls=%async_computation.7 | async-start | bytes 8388608
  202.6 24.5 %copy-start.10 = (f32[1024,1024]{1,0:T(8,128)}, f32[1024,1024]{1,0:T(8,128)S(1)}, u32[]{:S(2)}) copy-start(f32[1024,1024]{1,0:T(8,128)S(1)} %divide_select_fusion.3) | copy-start | bytes 12582916
  202.6 10.5 %slice-start.2 = ((s8[16777216]{0:T(1024)(128)(4,1)}), s8[4194304]{0:T(1024)(128)(4,1)S(1)}, s32[]{:S(2)}) async-start(s8[16777216]{0:T(1024)(128)(4,1)} %bitcast.33), calls=%async_computation.8 | async-start | bytes 8388608
  202.7 10.5 %slice-start.3 = ((s8[16777216]{0:T(1024)(128)(4,1)}), s8[4194304]{0:T(1024)(128)(4,1)S(1)}, s32[]{:S(2)}) async-start(s8[16777216]{0:T(1024)(128)(4,1)} %bitcast.33), calls=%async_computation.9 | async-start | bytes 8388608
  213.1 17.5 %copy-start.8 = (f32[1024,1024]{1,0:T(8,128)}, f32[1024,1024]{1,0:T(8,128)S(1)}, u32[]{:S(2)}) copy-start(f32[1024,1024]{1,0:T(8,128)S(1)} %divide_select_fusion.2) | copy-start | bytes 12582916
  219.9 14.0 %copy-start.6 = (f32[1024,1024]{1,0:T(8,128)}, f32[1024,1024]{1,0:T(8,128)S(1)}, u32[]{:S(2)}) copy-start(f32[1024,1024]{1,0:T(8,128)S(1)} %divide_select_fusion.1) | copy-start | bytes 12582916
  219.9 7.1 %copy-start.3 = (f32[2048,256]{1,0:T(8,128)S(1)}, f32[2048,256]{1,0:T(8,128)}, u32[]{:S(2)}) copy-start(f32[2048,256]{1,0:T(8,128)} %all-gather.3.cloned.1.call-done) | copy-start | bytes 6291460
  226.9 10.7 %copy-start.4 = (f32[1024,1024]{1,0:T(8,128)}, f32[1024,1024]{1,0:T(8,128)S(1)}, u32[]{:S(2)}) copy-start(f32[1024,1024]{1,0:T(8,128)S(1)} %divide_select_fusion) | copy-start | bytes 12582916
  242.5 203.9 %reduce-scatter.2.cloned.1.call-start = ((), (), s32[]{:S(2)}) async-start(), calls=%async_computation.3 | async-start | bytes 2359296 | tf_op jit(solution)/shard_map/reduce_scatter | solution.py:92
  242.5 9.5 %copy-start.9 = (f32[1024,1024]{1,0:T(8,128)S(1)}, f32[1024,1024]{1,0:T(8,128)}, u32[]{:S(2)}) copy-start(f32[1024,1024]{1,0:T(8,128)} %copy-done.8) | copy-start | bytes 12582916
  242.5 9.5 %copy-start.12 = (f32[2048,256]{1,0:T(8,128)S(1)}, f32[2048,256]{1,0:T(8,128)}, u32[]{:S(2)}) copy-start(f32[2048,256]{1,0:T(8,128)} %all-reduce.4.cloned.1.call-done) | copy-start | bytes 6291460
  252.0 7.0 %copy-start.7 = (f32[1024,1024]{1,0:T(8,128)S(1)}, f32[1024,1024]{1,0:T(8,128)}, u32[]{:S(2)}) copy-start(f32[1024,1024]{1,0:T(8,128)} %copy-done.6) | copy-start | bytes 12582916
  259.0 7.1 %copy-start.5 = (f32[1024,1024]{1,0:T(8,128)S(1)}, f32[1024,1024]{1,0:T(8,128)}, u32[]{:S(2)}) copy-start(f32[1024,1024]{1,0:T(8,128)} %copy-done.4) | copy-start | bytes 12582916
  273.1 266.9 %copy-start.13 = (f32[256,256]{1,0:T(8,128)S(1)}, f32[256,256]{1,0:T(8,128)}, u32[]{:S(2)}) copy-start(f32[256,256]{1,0:T(8,128)} %param.8) | copy-start | bytes 786436
  273.1 266.9 %copy-start.14 = (f32[256,256]{1,0:T(8,128)S(1)}, f32[256,256]{1,0:T(8,128)}, u32[]{:S(2)}) copy-start(f32[256,256]{1,0:T(8,128)} %param.9) | copy-start | bytes 786436
  274.5 265.6 %all-reduce.8.cloned.1.call-start = ((), (), s32[]{:S(2)}) async-start(), calls=%async_computation.5 | async-start | bytes 4194304 | tf_op jit(solution)/shard_map/psum | solution.py:15
  (2 other events, 2.7 us)
Sparse Core Ops, SparseCore 0:
  10.4 57.4 all-gather.2
  71.2 121.8 all-reduce.3
  242.6 123.9 all-reduce.5
  370.2 76.0 reduce-scatter.1
  448.9 91.0 all-reduce.7
where the time goes:
time: 558 us; the launch traced here: 549 us
  waiting for transfers between devices  344 us (62%)
  blocking collectives  93.7 us (17%)
  matrix products  77.9 us (14%)
  between operations  20.3 us (4%)
  other arithmetic  8.8 us (2%)
    psum x2, waiting for transfers between devices, broadcast(): return lax.psum(jnp.where(mine, array, jnp.zeros_like(array)), axis)  115 us
    psum x1, waiting for transfers between devices, local(): row_sums = lax.psum(row_part, 'col')  92.1 us
    reduce_scatter x1, waiting for transfers between devices, local(): owned = lax.psum_scatter(col_part, 'row', scatter_dimension=0, tiled=True)  76.6 us
    psum x1, blocking collectives, local(): lax.psum(jnp.sum(marginal.astype(jnp.float32)), ('row', 'col'))  63.3 us
    all_gather x1, waiting for transfers between devices, local(): lax.all_gather(embed, 'row', axis=0, tiled=True)  59.9 us
    dot_general x4, matrix products, tile_grads(): lax.dot_general(row_vecs, col_vecs, (((1,), (1,)), ((), ())), precision=l...  33.6 us
    dot_general x4, matrix products, tile_grads(): lax.dot_general(slopes, row_vecs, (((0,), (0,)), ((), ())), precision=lax...  30.3 us
    all_gather x1, blocking collectives, local(): lax.all_gather(marginal, 'row', axis=0, tiled=True)  19.2 us
  transfers between devices with their start and end apart: 5, of which 5 were waited for; matrix products, arithmetic and copies ran while one was open for 6% of the time, Pallas kernels for 0%

commit v1 on v0

v1 whole, which is shorter than its diff:
```python
import functools

import jax
import jax.numpy as jnp
from jax import lax
from jax.experimental import pallas as pl
from jax.experimental.pallas import tpu as pltpu
from jax.sharding import PartitionSpec as P

LEARN_RATE = 0.05
MESH = pl.DeviceIdType.MESH
PAD = 8
RING = 4
N_SEND = 80
N_RECV = 64


def split(value):
    high = value.astype(jnp.bfloat16)
    low = (value - high.astype(jnp.float32)).astype(jnp.bfloat16)
    return high, low


class Copies:
    def __init__(self, send_sems, recv_sems):
        self.send_sems, self.recv_sems = send_sems, recv_sems
        self.sends = self.recvs = 0
        self.pending = []

    def send_sem(self):
        self.sends += 1
        return self.send_sems.at[self.sends - 1]

    def recv_sem(self, count=1):
        self.recvs += count
        return self.recvs - count

    def start(self, src, dst, device):
        copy = pltpu.make_async_remote_copy(
            src_ref=src,
            dst_ref=dst,
            send_sem=self.send_sem(),
            recv_sem=self.recv_sems.at[self.recv_sem()],
            device_id=device,
            device_id_type=MESH,
        )
        copy.start()
        self.pending.append(copy)
        return copy

    def finish(self):
        for copy in self.pending:
            copy.wait_send()


def kernel(
    block,
    embed_hbm,
    marg_ref,
    tiles_ref,
    accum_hbm,
    cooc_hbm,
    new_embed_ref,
    new_accum_ref,
    col_land,
    row_land,
    row_src,
    cooc_v,
    accum_v,
    e_hi,
    e_lo,
    et_hi,
    et_lo,
    c_hi,
    c_lo,
    row_log,
    col_log,
    row_grad,
    col_grad,
    sib_in,
    row_in1,
    row_in2,
    row_in3,
    row_in4,
    col_in1,
    col_in2,
    col_in3,
    tot1,
    tot2,
    tot3,
    send_sems,
    recv_sems,
    local_sems,
):
    share, width = embed_hbm.shape
    half = share // 2
    row = lax.axis_index("row")
    col = lax.axis_index("col")
    zh, y = row // 4, lax.rem(row, 4)
    x, zl, q = col // 4, lax.rem(col // 2, 2), lax.rem(col, 2)

    def device(zh_=zh, y_=y, x_=x, zl_=zl, q_=q):
        return (zh_ * 4 + y_, x_ * 4 + zl_ * 2 + q_)

    def ring(position, step):
        return lax.rem(position + step + RING, RING)

    x_up, x_down, x_far = ring(x, 1), ring(x, -1), ring(x, 2)
    y_up, y_down, y_far = ring(y, 1), ring(y, -1), ring(y, 2)
    is_owner = col < 8

    def flip(bit, by):
        return 1 - bit if by else bit

    near = [
        device(zh_=flip(zh, k // 4), zl_=flip(zl, k // 2 % 2), q_=flip(q, k % 2))
        for k in range(1, 8)
    ]
    near_y = [device(y_=ring(y, k)) for k in range(1, 4)]
    near_x = [device(x_=ring(x, k)) for k in range(1, 4)]
    sibling, zl_pair, zh_pair = near[0], near[1], near[3]
    source = (zl * 4 + ring(x, -1), row)
    targets = [(col, ring(y, 1) * 4 + zh * 2 + k) for k in range(2)]

    embed_in = pltpu.make_async_copy(
        embed_hbm, col_land.at[zh, y, pl.ds(0, share)], local_sems.at[0]
    )
    embed_in.start()
    accum_in = pltpu.make_async_copy(accum_hbm, accum_v, local_sems.at[1])
    accum_in.start()
    cooc_in = []
    for p in range(8):
        copy = pltpu.make_async_copy(
            cooc_hbm.at[pl.ds(p * share, share)],
            cooc_v.at[pl.ds(p * share, share)],
            local_sems.at[2 + p],
        )
        copy.start()
        cooc_in.append(copy)

    barrier = pltpu.get_barrier_semaphore()
    for other in near + near_y + near_x + [source]:
        pl.semaphore_signal(barrier, inc=1, device_id=other, device_id_type=MESH)

    @pl.when(is_owner)
    def _():
        for other in targets:
            pl.semaphore_signal(barrier, inc=1, device_id=other, device_id_type=MESH)

    marg = marg_ref[...].astype(jnp.float32)
    logs = jnp.log(marg)
    tot1[0] = jnp.broadcast_to(jnp.sum(marg, axis=1, keepdims=True), tot1.shape[1:])

    @pl.when(is_owner)
    def _():
        pl.semaphore_wait(barrier, 16)

    @pl.when(jnp.logical_not(is_owner))
    def _():
        pl.semaphore_wait(barrier, 14)

    net = Copies(send_sems, recv_sems)

    def spread(block_ref, others):
        sem = recv_sems.at[net.recv_sem()]
        count = len(others)
        for k, other in enumerate(others):
            copy = pltpu.make_async_remote_copy(
                src_ref=block_ref.at[0],
                dst_ref=block_ref.at[k + 1],
                send_sem=net.send_sem(),
                recv_sem=sem,
                device_id=other,
                device_id_type=MESH,
            )
            copy.start()
            net.pending.append(copy)
        landed = block_ref.at[pl.ds(1, count)]
        return pltpu.make_async_copy(landed, landed, sem)

    stage1 = spread(tot1, near)

    embed_in.wait()
    col_land[zh, y, pl.ds(share, PAD), :] = jnp.broadcast_to(logs, (PAD, width))
    for h in range(2):
        row_src[h, pl.ds(0, half), :] = col_land[zh, y, pl.ds(h * half, half), :]
        row_src[h, pl.ds(half, PAD), :] = jnp.broadcast_to(
            jnp.concatenate([logs[:, h * half : (h + 1) * half]] * 2, axis=1), (PAD, width)
        )
    scatter_recv = recv_sems.at[net.recv_sem()]
    scatter = [
        pltpu.make_async_remote_copy(
            src_ref=row_src.at[k],
            dst_ref=row_land.at[zh, y_up, k],
            send_sem=net.send_sem(),
            recv_sem=scatter_recv,
            device_id=targets[k],
            device_id_type=MESH,
        )
        for k in range(2)
    ]

    @pl.when(is_owner)
    def _():
        for copy in scatter:
            copy.start()

    def whole(land, index):
        return land.at[index]

    def first(land, index):
        return land.at[(*index, pl.ds(0, land.shape[-2] // 16 * 8 + PAD))]

    def second(land, index):
        start = land.shape[-2] // 16 * 8 + PAD
        return land.at[(*index, pl.ds(start, land.shape[-2] - start))]

    def send(view, land, index, other):
        part = view(land, index)
        return net.start(part, part, other)

    c0, c1 = zh, 1 - zh
    near_pair = send(whole, col_land, (c0, y), zh_pair)
    col_up = send(whole, col_land, (c0, y), near_y[0])
    col_down = send(whole, col_land, (c0, y), near_y[2])

    stage1.wait()
    tot2[0] = jnp.sum(tot1[...], axis=0)
    stage2 = spread(tot2, near_y)

    r0, r1 = zl, 1 - zl
    scatter[0].wait_recv()
    row_pair = send(whole, row_land, (r0, x, q), zl_pair)
    row_up = send(whole, row_land, (r0, x, q), near_x[0])
    row_down = send(whole, row_land, (r0, x, q), near_x[2])
    sib = [send(whole, row_land, (r0, x, q), sibling)]

    stage2.wait()
    tot3[0] = jnp.sum(tot2[...], axis=0)
    stage3 = spread(tot3, near_x)

    col_up.wait_recv()
    col_far_up = send(first, col_land, (c0, y_down), near_y[0])
    col_down.wait_recv()
    col_far_down = send(second, col_land, (c0, y_up), near_y[2])

    row_up.wait_recv()
    row_far_up = send(first, row_land, (r0, x_down, q), near_x[0])
    sib.append(send(whole, row_land, (r0, x_down, q), sibling))
    row_down.wait_recv()
    row_far_down = send(second, row_land, (r0, x_up, q), near_x[2])
    sib.append(send(whole, row_land, (r0, x_up, q), sibling))

    row_pair.wait_recv()
    row_up = send(whole, row_land, (r1, x, q), near_x[0])
    row_down = send(whole, row_land, (r1, x, q), near_x[2])
    sib.append(send(whole, row_land, (r1, x, q), sibling))

    near_pair.wait_recv()
    col_up = send(whole, col_land, (c1, y), near_y[0])
    col_down = send(whole, col_land, (c1, y), near_y[2])

    stage3.wait()
    log_total = jnp.log(jnp.sum(tot3[...], axis=0))[:1, :1]

    row_far_up.wait_recv()
    row_far_down.wait_recv()
    sib.append(send(whole, row_land, (r0, x_far, q), sibling))
    row_up.wait_recv()
    row_far_up = send(first, row_land, (r1, x_down, q), near_x[0])
    sib.append(send(whole, row_land, (r1, x_down, q), sibling))
    row_down.wait_recv()
    row_far_down = send(second, row_land, (r1, x_up, q), near_x[2])
    sib.append(send(whole, row_land, (r1, x_up, q), sibling))

    col_far_up.wait_recv()
    col_far_down.wait_recv()
    col_up.wait_recv()
    col_far_up = send(first, col_land, (c1, y_down), near_y[0])
    col_down.wait_recv()
    col_far_down = send(second, col_land, (c1, y_up), near_y[2])

    row_far_up.wait_recv()
    row_far_down.wait_recv()
    sib.append(send(whole, row_land, (r1, x_far, q), sibling))
    for copy in sib:
        copy.wait_recv()
    col_far_up.wait_recv()
    col_far_down.wait_recv()

    def convert(p, carry):
        g, w = p // 4, lax.rem(p, 4)
        rows = pl.ds(pl.multiple_of(p * share, share), share)
        c_hi[rows, :], c_lo[rows, :] = split(col_land[g, w, pl.ds(0, share), :])
        col_log[p] = col_land[g, w, pl.ds(share, PAD), :] - log_total
        at = ring(w, 1)
        piece = jnp.concatenate(
            [row_land[g, at, 0, pl.ds(0, half), :], row_land[g, at, 1, pl.ds(0, half), :]], axis=0
        )
        e_hi[rows, :], e_lo[rows, :] = split(piece)
        flipped = piece.T
        et_hi[p], et_lo[p] = split(flipped)
        for h in range(2):
            line = row_land[g, at, h, pl.ds(half, 1), pl.ds(0, half)]
            row_log[pl.ds(pl.multiple_of(p * share + h * half, half), half), :] = jnp.broadcast_to(
                line, (128, half)
            ).T
        return carry

    lax.fori_loop(0, 8, convert, 0)

    row_grad[...] = jnp.zeros_like(row_grad)
    col_grad[...] = jnp.zeros_like(col_grad)
    for copy in cooc_in:
        copy.wait()

    entries = [tiles_ref[0, k] for k in range(4)]

    def listed(t):
        on = [jnp.where(entry == t, jnp.float32(1), jnp.float32(0)) for entry in entries]
        return (on[0] + on[1]) + (on[2] + on[3])

    def chunk(step, carry):
        p, j = step // 2, lax.rem(step, 2)
        on = listed(p // 4 * 2 + j)
        rows = pl.ds(pl.multiple_of(p * share, share), share)
        eh = e_hi[rows, :]
        rows_cat = jnp.concatenate([eh, eh, e_lo[rows, :]], axis=1)
        th = et_hi[p]
        flipped_cat = jnp.concatenate([th, et_lo[p], th], axis=1)
        logs_row = jnp.concatenate([row_log[rows, :]] * (share // 128), axis=1)
        to_rows = jnp.zeros((share, width), jnp.float32)
        for k in range(4):
            pc = j * 4 + k
            cols = pl.ds(pl.multiple_of(pc * share, share), share)
            ch, cl = c_hi[cols, :], c_lo[cols, :]
            scores = lax.dot_general(
                rows_cat,
                jnp.concatenate([ch, cl, ch], axis=1),
                (((1,), (1,)), ((), ())),
                preferred_element_type=jnp.float32,
            )
            centred = scores + logs_row + col_log[pc, :1, :]
            counts = cooc_v[rows, cols]
            counts_f = jnp.maximum(counts.astype(jnp.float32), 1.0)
            slopes = on * jnp.where(
                counts > 0,
                (0.1 + 0.25 * jnp.sqrt(counts_f)) * (centred - jnp.log(counts_f)),
                1.0 / (1.0 + jnp.exp(-centred)),
            )
            sh, sl = split(slopes)
            to_rows += jnp.dot(
                jnp.concatenate([sh, sh, sl], axis=1),
                jnp.concatenate([ch, cl, ch], axis=0),
                preferred_element_type=jnp.float32,
            )
            col_grad[j, k] += jnp.dot(
                flipped_cat,
                jnp.concatenate([sh, sh, sl], axis=0),
                preferred_element_type=jnp.float32,
            )
        at = ring(lax.rem(p, 4), 1)
        for h in range(2):
            row_grad[h, p // 4, at] += to_rows[h * half : (h + 1) * half]
        return carry

    lax.fori_loop(0, 16, chunk, 0)

    from_sib = net.start(row_grad.at[1 - q], sib_in, sibling)

    def col_part(index, upper):
        return col_grad.at[index[0], index[1], pl.ds(upper * (width // 2), width // 2)]

    def row_part(g, at, upper):
        return row_grad.at[q, g, at, pl.ds(upper * (half // 2), half // 2)]

    col_first = [
        (
            net.start(col_part((g, y_far), 0), col_in1.at[0, g], near_y[0]),
            net.start(col_part((g, y_far), 1), col_in1.at[1, g], near_y[2]),
        )
        for g in range(2)
    ]
    from_sib.wait_recv()
    row_grad[q] += sib_in[...]
    row_first = [
        (
            net.start(row_part(g, x_far, 0), row_in1.at[0, g], near_x[0]),
            net.start(row_part(g, x_far, 1), row_in1.at[1, g], near_x[2]),
        )
        for g in range(2)
    ]
    col_second, row_second = [], []
    for g in range(2):
        for copy in col_first[g]:
            copy.wait_recv()
        col_grad[g, y_up, pl.ds(0, width // 2), :] += col_in1[0, g]
        up = net.start(col_grad.at[g, y_up], col_in2.at[0, g], near_y[0])
        col_grad[g, y_down, pl.ds(width // 2, width // 2), :] += col_in1[1, g]
        down = net.start(col_grad.at[g, y_down], col_in2.at[1, g], near_y[2])
        col_second.append((up, down))
    for g in range(2):
        for copy in row_first[g]:
            copy.wait_recv()
        row_grad[q, g, x_up, pl.ds(0, half // 2), :] += row_in1[0, g]
        up = net.start(row_grad.at[q, g, x_up], row_in2.at[0, g], near_x[0])
        row_grad[q, g, x_down, pl.ds(half // 2, half // 2), :] += row_in1[1, g]
        down = net.start(row_grad.at[q, g, x_down], row_in2.at[1, g], near_x[2])
        row_second.append((up, down))
    for g in range(2):
        for copy in row_second[g]:
            copy.wait_recv()
        row_grad[q, g, x] += row_in2[0, g] + row_in2[1, g]
    row_last = net.start(row_grad.at[q, 1 - zl, x], row_in3, zl_pair)
    for g in range(2):
        for copy in col_second[g]:
            copy.wait_recv()
        col_grad[g, y] += col_in2[0, g] + col_in2[1, g]
    col_last = net.start(col_grad.at[1 - zh, y], col_in3, zh_pair)
    row_last.wait_recv()
    row_grad[q, zl, x] += row_in3[...]
    home_sem = net.recv_sem(2)
    home = pltpu.make_async_remote_copy(
        src_ref=row_grad.at[q, zl, x],
        dst_ref=row_in4.at[q],
        send_sem=net.send_sem(),
        recv_sem=recv_sems.at[home_sem + q],
        device_id=source,
        device_id_type=MESH,
    )
    home.start()
    net.pending.append(home)
    col_last.wait_recv()
    own = (col_grad[zh, y] + col_in3[...]).T
    accum_in.wait()

    def update(gradient):
        gradients = gradient * (1.0 / block)
        accum = accum_v[...] + gradients * gradients
        new_accum_ref[...] = accum
        new_embed_ref[...] = (
            col_land[zh, y, pl.ds(0, share), :] - LEARN_RATE * gradients / jnp.sqrt(accum)
        )

    @pl.when(is_owner)
    def _():
        for h in range(2):
            pltpu.make_async_copy(
                row_in4.at[h], row_in4.at[h], recv_sems.at[home_sem + h]
            ).wait()
        update(own + jnp.concatenate([row_in4[0], row_in4[1]], axis=0))
        for copy in scatter:
            copy.wait_send()

    @pl.when(jnp.logical_not(is_owner))
    def _():
        update(own)

    net.finish()


def local(cooc, tile_list, marginal, embed, accum):
    share, width = embed.shape
    half = share // 2
    items = 8 * share
    f32, bf16 = jnp.float32, jnp.bfloat16
    hbm = pl.BlockSpec(memory_space=pl.ANY)
    vmem = pl.BlockSpec(memory_space=pltpu.VMEM)
    smem = pl.BlockSpec(memory_space=pltpu.SMEM)
    shape = jax.ShapeDtypeStruct((share, width), f32)
    return pl.pallas_call(
        functools.partial(kernel, items // 2),
        out_shape=(shape, shape),
        in_specs=[hbm, vmem, smem, hbm, hbm],
        out_specs=(vmem, vmem),
        scratch_shapes=[
            pltpu.VMEM((2, 4, share + PAD, width), f32),
            pltpu.VMEM((2, 4, 2, half + PAD, width), f32),
            pltpu.VMEM((2, half + PAD, width), f32),
            pltpu.VMEM((items, items), jnp.int32),
            pltpu.VMEM((share, width), f32),
            pltpu.VMEM((items, width), bf16),
            pltpu.VMEM((items, width), bf16),
            pltpu.VMEM((8, width, share), bf16),
            pltpu.VMEM((8, width, share), bf16),
            pltpu.VMEM((items, width), bf16),
            pltpu.VMEM((items, width), bf16),
            pltpu.VMEM((items, 128), f32),
            pltpu.VMEM((8, PAD, share), f32),
            pltpu.VMEM((2, 2, 4, half, width), f32),
            pltpu.VMEM((2, 4, width, share), f32),
            pltpu.VMEM((2, 4, half, width), f32),
            pltpu.VMEM((2, 2, half // 2, width), f32),
            pltpu.VMEM((2, 2, half, width), f32),
            pltpu.VMEM((half, width), f32),
            pltpu.VMEM((2, half, width), f32),
            pltpu.VMEM((2, 2, width // 2, share), f32),
            pltpu.VMEM((2, 2, width, share), f32),
            pltpu.VMEM((width, share), f32),
            pltpu.VMEM((8, 8, 128), f32),
            pltpu.VMEM((4, 8, 128), f32),
            pltpu.VMEM((4, 8, 128), f32),
            pltpu.SemaphoreType.DMA((N_SEND,)),
            pltpu.SemaphoreType.DMA((N_RECV,)),
            pltpu.SemaphoreType.DMA((10,)),
        ],
        compiler_params=pltpu.CompilerParams(
            collective_id=0, has_side_effects=True, vmem_limit_bytes=56 * 2**20
        ),
        cost_estimate=pl.CostEstimate(
            flops=18 * items * items * width, bytes_accessed=4 * items * items, transcendentals=0
        ),
    )(embed, marginal.reshape(1, share), tile_list.reshape(1, 4), accum, cooc)


def solution(mesh):
    placed = (
        P("row", "col"),
        P("row", "col", None),
        P(("col", "row")),
        P(("col", "row"), None),
        P(("col", "row"), None),
    )
    return jax.shard_map(
        local,
        mesh=mesh,
        in_specs=placed,
        out_specs=(P(("col", "row"), None), P(("col", "row"), None)),
        check_vma=False,
    )
```

time: 558 us -> 121 us (0.22)
  the two profiles are of different devices: /device:TPU:0 before, /device:TPU:26 now
where the time goes in v1:
time: 121 us; the launch traced here: 120 us
  Pallas kernels  116 us (96%)
  local copies, waits for them, and re-layouts  3.34 us (3%)
    pallas_call x1, Pallas kernels, local(): pl.pallas_call(functools.partial(kernel, items // 2), out_shape=(shape, s...  116 us
    unnamed x2, local copies, waits for them, and re-layouts  3.34 us

profile of v1, /device:TPU:26, one launch (start us, length us, event | category | flops | bytes accessed | tf_op | source)
XLA Modules:
  0.0 119.9 jit_solution(7170151023762027)
XLA Ops:
  0.6 115.9 %shard_map.68 = (f32[256,256]{1,0:T(8,128)}, f32[256,256]{1,0:T(8,128)}) custom-call(f32[256,256]{1,0:T(8,128)} %embed_hbm.1, s32[1,256]{1,0:T(1,128)} %bitcast.2, s32[1,4]{1,0:T(1,128)} %bitcast.3, f32[256,256]{1,0:T(8,128)} %accum_hbm.1, s32[2048,2048]{1,0:T(8,128)} %cooc_hbm.1), custom_call_target="tpu_custom_call" | custom-call | flops 19327352832 | bytes 16777216 | tf_op jit(solution)/shard_map/pallas_call | solution.py:471
  116.5 1.7 %copy.9 = f32[256,256]{1,0:T(8,128)} copy(f32[256,256]{1,0:T(8,128)} %get-tuple-element.4) | data formatting | bytes 524288
  118.2 1.7 %copy.10 = f32[256,256]{1,0:T(8,128)} copy(f32[256,256]{1,0:T(8,128)} %get-tuple-element.5) | data formatting | bytes 524288

commit v2 on v0

v2 whole, which is shorter than its diff:
```python
import jax
import jax.numpy as jnp
from jax import lax
from jax.experimental import pallas as pl
from jax.experimental.pallas import tpu as pltpu
from jax.sharding import PartitionSpec as P

LEARN_RATE = 0.05
MESH = pl.DeviceIdType.MESH
PAD = 8
RING = 4
N_SEND = 64
N_RECV = 48


def split(value):
    high = value.astype(jnp.bfloat16)
    low = (value - high.astype(jnp.float32)).astype(jnp.bfloat16)
    return high, low


class Copies:
    def __init__(self, send_sems, recv_sems):
        self.send_sems, self.recv_sems = send_sems, recv_sems
        self.sends = self.recvs = 0
        self.pending = []

    def send_sem(self):
        self.sends += 1
        return self.send_sems.at[self.sends - 1]

    def recv_sem(self, count=1):
        self.recvs += count
        return self.recvs - count

    def make(self, src, dst, device):
        copy = pltpu.make_async_remote_copy(
            src_ref=src,
            dst_ref=dst,
            send_sem=self.send_sem(),
            recv_sem=self.recv_sems.at[self.recv_sem()],
            device_id=device,
            device_id_type=MESH,
        )
        self.pending.append(copy)
        return copy

    def finish(self):
        for copy in self.pending:
            copy.wait_send()


def kernel(
    embed_hbm,
    marg_ref,
    tiles_ref,
    cooc_hbm,
    grad_ref,
    col_land,
    row_land,
    row_src,
    cooc_v,
    e_hi,
    e_lo,
    et_hi,
    et_lo,
    c_hi,
    c_lo,
    row_log,
    col_log,
    scores_v,
    row_grad,
    col_grad,
    sib_in,
    row_in,
    row_home,
    col_in,
    col_last,
    tot1,
    tot2,
    tot3,
    send_sems,
    recv_sems,
    local_sems,
):
    share, width = embed_hbm.shape
    half = share // 2
    row = lax.axis_index("row")
    col = lax.axis_index("col")
    zh, y = row // 4, lax.rem(row, 4)
    x, zl, q = col // 4, lax.rem(col // 2, 2), lax.rem(col, 2)

    def device(zh_=zh, y_=y, x_=x, zl_=zl, q_=q):
        return (zh_ * 4 + y_, x_ * 4 + zl_ * 2 + q_)

    def ring(position, step):
        return lax.rem(position + step + RING, RING)

    def offset(o):
        return jnp.where(o == 0, 2, jnp.where(o == 1, 1, jnp.where(o == 2, 3, 0)))

    is_owner = col < 8

    def flip(bit, by):
        return 1 - bit if by else bit

    near = [
        device(zh_=flip(zh, k // 4), zl_=flip(zl, k // 2 % 2), q_=flip(q, k % 2))
        for k in range(1, 8)
    ]
    near_y = [device(y_=ring(y, k)) for k in range(1, 4)]
    near_x = [device(x_=ring(x, k)) for k in range(1, 4)]
    by_y = [near_y[1], near_y[0], near_y[2]]
    by_x = [near_x[1], near_x[0], near_x[2]]
    sibling, zl_pair, zh_pair = near[0], near[1], near[3]
    blocks = [lax.rem(zh + zl + s + y // 2, 2) for s in range(2)]

    def piece_y(x_):
        return lax.rem(zh + 1 + y - x_ + RING, RING)

    source = [(blocks[s] * 4 + piece_y(x), row) for s in range(2)]
    x_place = lax.rem(x + 1 - y + zl * 2 + q + RING, RING)
    zl_place = lax.rem(zl + zh + x, 2)
    targets = [
        [(col, x_place * 4 + lax.rem(zl_place + s, 2) * 2 + k) for k in range(2)] for s in range(2)
    ]

    embed_in = pltpu.make_async_copy(
        embed_hbm, col_land.at[zh, y, pl.ds(0, share)], local_sems.at[0]
    )
    embed_in.start()
    cooc_in = []
    for p in range(8):
        copy = pltpu.make_async_copy(
            cooc_hbm.at[pl.ds(p * share, share)],
            cooc_v.at[pl.ds(p * share, share)],
            local_sems.at[1 + p],
        )
        copy.start()
        cooc_in.append(copy)

    def signal(other):
        pl.semaphore_signal(barrier, inc=1, device_id=other, device_id_type=MESH)

    barrier = pltpu.get_barrier_semaphore()
    for other in near + near_y + near_x + [source[0]]:
        signal(other)

    @pl.when(is_owner)
    def _():
        for s in range(2):
            for other in targets[s]:
                signal(other)

    marg = marg_ref[...].astype(jnp.float32)
    logs = jnp.log(marg)
    tot1[0] = jnp.broadcast_to(jnp.sum(marg, axis=1, keepdims=True), tot1.shape[1:])
    embed_in.wait()
    col_land[zh, y, pl.ds(share, PAD), :] = jnp.broadcast_to(logs, (PAD, width))
    for h in range(2):
        row_src[h, pl.ds(0, half), :] = col_land[zh, y, pl.ds(h * half, half), :]
        row_src[h, pl.ds(half, PAD), :] = jnp.broadcast_to(
            jnp.concatenate([logs[:, h * half : (h + 1) * half]] * 2, axis=1), (PAD, width)
        )

    pl.semaphore_wait(barrier, 15 + jnp.where(is_owner, 2, 0))

    net = Copies(send_sems, recv_sems)

    def spread(block_ref, others):
        sem = recv_sems.at[net.recv_sem()]
        for k, other in enumerate(others):
            copy = pltpu.make_async_remote_copy(
                src_ref=block_ref.at[0],
                dst_ref=block_ref.at[k + 1],
                send_sem=net.send_sem(),
                recv_sem=sem,
                device_id=other,
                device_id_type=MESH,
            )
            copy.start()
            net.pending.append(copy)
        landed = block_ref.at[pl.ds(1, len(others))]
        return pltpu.make_async_copy(landed, landed, sem)

    def same(ref, other):
        return net.make(ref, ref, other)

    def start(copies):
        for copy in copies:
            copy.start()

    def arrive(copies):
        for copy in copies:
            copy.wait_recv()

    zls, zhs = (zl, 1 - zl), (zh, 1 - zh)
    scatter_recv = recv_sems.at[net.recv_sem()]
    scatter = [
        pltpu.make_async_remote_copy(
            src_ref=row_src.at[k],
            dst_ref=row_land.at[zl_place, k, x_place],
            send_sem=net.send_sem(),
            recv_sem=scatter_recv,
            device_id=targets[0][k],
            device_id_type=MESH,
        )
        for k in range(2)
    ]
    col_pair = same(col_land.at[zh, y], zh_pair)
    row_pair = same(row_land.at[zl, q, x], zl_pair)
    col_out = [[same(col_land.at[zhs[s], y], other) for other in by_y] for s in range(2)]
    row_out = [[same(row_land.at[zls[s], q, x], other) for other in by_x] for s in range(2)]
    sib_out = [same(row_land.at[zls[s], q], sibling) for s in range(2)]
    sib_parts = [(1, 0, 4), (0, 0, 2), (0, 2, 2)]
    sib_back = [
        net.make(row_grad.at[1 - q, s, pl.ds(a, n)], sib_in.at[s, pl.ds(a, n)], sibling)
        for s, a, n in sib_parts
    ]
    col_back = [
        [net.make(col_grad.at[s, o], col_in.at[s, o], by_y[o]) for o in range(3)] for s in range(2)
    ]
    row_back = [
        [net.make(row_grad.at[q, s, o], row_in.at[s, o], by_x[o]) for o in range(3)]
        for s in range(2)
    ]
    pair_back = net.make(col_grad.at[1, 3], col_last, zh_pair)
    home_sem = net.recv_sem(4)
    home = [
        pltpu.make_async_remote_copy(
            src_ref=row_grad.at[q, s, 3],
            dst_ref=row_home.at[s, q],
            send_sem=net.send_sem(),
            recv_sem=recv_sems.at[home_sem + 2 * s + q],
            device_id=source[s],
            device_id_type=MESH,
        )
        for s in range(2)
    ]

    stage1 = spread(tot1, near)

    @pl.when(is_owner)
    def _():
        start(scatter)

    start([col_pair, col_out[0][1], col_out[0][2], col_out[0][0]])
    stage1.wait()
    tot2[0] = jnp.sum(tot1[...], axis=0)
    stage2 = spread(tot2, near_x)
    scatter[0].wait_recv()
    start([row_pair, row_out[0][1], row_out[0][2], row_out[0][0]])
    stage2.wait()
    tot3[0] = jnp.sum(tot2[...], axis=0)
    stage3 = spread(tot3, near_y)
    row_grad[...] = jnp.zeros_like(row_grad)
    col_grad[...] = jnp.zeros_like(col_grad)
    col_pair.wait_recv()
    start(col_out[1])
    row_pair.wait_recv()
    start(row_out[1])
    stage3.wait()
    log_total = jnp.log(jnp.sum(tot3[...], axis=0))[:1, :1]

    def rows_of(index, count=1):
        return pl.ds(pl.multiple_of(index * share, share), count * share)

    def convert_cols(s):
        def piece(o, carry):
            at = ring(y, offset(o))
            index = s * 4 + o
            rows = rows_of(index)
            c_hi[rows, :], c_lo[rows, :] = split(col_land[zhs[s], at, pl.ds(0, share), :])
            col_log[index] = col_land[zhs[s], at, pl.ds(share, PAD), :] - log_total
            return carry

        lax.fori_loop(0, 4, piece, 0)

    def convert_rows(s):
        def piece(o, carry):
            at = ring(x, offset(o))
            index = s * 4 + o
            rows = rows_of(index)
            values = jnp.concatenate(
                [row_land[zls[s], h, at, pl.ds(0, half), :] for h in range(2)], axis=0
            )
            e_hi[rows, :], e_lo[rows, :] = split(values)
            et_hi[index], et_lo[index] = split(values.T)
            for h in range(2):
                line = row_land[zls[s], h, at, pl.ds(half, 1), pl.ds(0, half)]
                row_log[
                    pl.ds(pl.multiple_of(index * share + h * half, half), half), :
                ] = jnp.broadcast_to(line, (128, half)).T
            return carry

        lax.fori_loop(0, 4, piece, 0)

    arrive(row_out[0])
    sib_out[0].start()
    arrive(col_out[0])
    convert_cols(0)
    for copy in cooc_in:
        copy.wait()
    sib_out[0].wait_recv()
    convert_rows(0)

    entries = [tiles_ref[0, k] for k in range(4)]

    def listed(t):
        on = [jnp.where(entry == t, jnp.float32(1), jnp.float32(0)) for entry in entries]
        return (on[0] + on[1]) + (on[2] + on[3])

    def place(s):
        early = s < 8
        late = jnp.maximum(s - 8, 0)
        rs = jnp.where(early, s // 4, 1 - lax.rem(late // 2, 2))
        hr = jnp.where(early, lax.rem(s // 2, 2), lax.rem(late, 2))
        cs = jnp.where(early, 0, 1)
        hc = jnp.where(early, lax.rem(s, 2), late // 4)
        return rs, hr, cs, hc

    def score(s, slot):
        rs, hr, cs, hc = place(s)
        rows, cols = rows_of(rs * 4 + hr * 2, 2), rows_of(cs * 4 + hc * 2, 2)
        eh, ch = e_hi[rows, :], c_hi[cols, :]
        scores_v[slot] = lax.dot_general(
            jnp.concatenate([eh, eh, e_lo[rows, :]], axis=1),
            jnp.concatenate([ch, c_lo[cols, :], ch], axis=1),
            (((1,), (1,)), ((), ())),
            preferred_element_type=jnp.float32,
        )

    def work(s, slot):
        score(jnp.minimum(s + 1, 15), 1 - slot)
        rs, hr, cs, hc = place(s)
        zr, zc = jnp.where(rs == 0, blocks[0], blocks[1]), lax.rem(zh + cs, 2)
        first_row, first_col = rs * 4 + hr * 2, cs * 4 + hc * 2
        rows, cols = rows_of(first_row, 2), rows_of(first_col, 2)
        count_rows = [rows_of(zr * 4 + piece_y(ring(x, k))) for k in (2 + hr, 1 - hr)]
        count_cols = [rows_of(zc * 4 + ring(y, k)) for k in (2 + hc, 1 - hc)]
        counts = jnp.concatenate(
            [jnp.concatenate([cooc_v[r, c] for c in count_cols], axis=1) for r in count_rows],
            axis=0,
        )
        logs_row = jnp.concatenate([row_log[rows, :]] * (2 * share // 128), axis=1)
        logs_col = jnp.concatenate([col_log[first_col + k, :1, :] for k in range(2)], axis=1)
        centred = scores_v[slot] + logs_row + logs_col
        counts_f = jnp.maximum(counts.astype(jnp.float32), 1.0)
        slopes = listed(zr * 2 + zc) * jnp.where(
            counts > 0,
            (0.1 + 0.25 * jnp.sqrt(counts_f)) * (centred - jnp.log(counts_f)),
            1.0 / (1.0 + jnp.exp(-centred)),
        )
        sh, sl = split(slopes)
        ch = c_hi[cols, :]
        to_rows = jnp.dot(
            jnp.concatenate([sh, sh, sl], axis=1),
            jnp.concatenate([ch, c_lo[cols, :], ch], axis=0),
            preferred_element_type=jnp.float32,
        )
        for k in range(2):
            for h in range(2):
                start_at = k * share + h * half
                row_grad[h, rs, hr * 2 + k] += to_rows[start_at : start_at + half]
        th = jnp.concatenate([et_hi[first_row + k] for k in range(2)], axis=1)
        tl = jnp.concatenate([et_lo[first_row + k] for k in range(2)], axis=1)
        to_cols = jnp.dot(
            jnp.concatenate([th, tl, th], axis=1),
            jnp.concatenate([sh, sh, sl], axis=0),
            preferred_element_type=jnp.float32,
        )
        for k in range(2):
            col_grad[cs, hc * 2 + k] += to_cols[:, k * share : (k + 1) * share]

    def before2():
        arrive(row_out[1])
        sib_out[1].start()

    def before3():
        sib_out[1].wait_recv()
        convert_rows(1)

    def before7():
        arrive(col_out[1])
        convert_cols(1)

    def before8():
        start(col_back[0])

    def before12():
        start(col_back[1][:2])

    def before14():
        sib_back[0].start()

    def before15():
        sib_back[1].start()
        sib_back[0].wait_recv()
        row_grad[q, 1] += sib_in[1]
        start(row_back[1])

    events = {2: before2, 3: before3, 7: before7, 8: before8, 12: before12, 14: before14, 15: before15}

    score(0, 0)

    def pair(i, carry):
        for u in range(2):
            for s, event in events.items():
                if s % 2 == u:
                    pl.when(i == s // 2)(event)
            work(2 * i + u, u)
        return carry

    lax.fori_loop(0, 8, pair, 0)

    sib_back[2].start()
    col_back[1][2].start()
    sib_back[1].wait_recv()
    row_grad[q, 0, pl.ds(0, 2)] += sib_in[0, pl.ds(0, 2)]
    start(row_back[0][:2])
    sib_back[2].wait_recv()
    row_grad[q, 0, pl.ds(2, 2)] += sib_in[0, pl.ds(2, 2)]
    row_back[0][2].start()
    arrive(col_back[0])
    col_grad[0, 3] += (col_in[0, 0] + col_in[0, 1]) + col_in[0, 2]
    arrive(row_back[1])
    row_grad[q, 1, 3] += (row_in[1, 0] + row_in[1, 1]) + row_in[1, 2]

    home[1].start()
    arrive(row_back[0])
    row_grad[q, 0, 3] += (row_in[0, 0] + row_in[0, 1]) + row_in[0, 2]
    home[0].start()
    arrive(col_back[1])
    col_grad[1, 3] += (col_in[1, 0] + col_in[1, 1]) + col_in[1, 2]
    pair_back.start()
    pair_back.wait_recv()
    grad_ref[...] = (col_grad[0, 3] + col_last[...]).T

    @pl.when(is_owner)
    def _():
        for s in range(2):
            for k in range(2):
                slot = row_home.at[s, k]
                pltpu.make_async_copy(slot, slot, recv_sems.at[home_sem + 2 * s + k]).wait()
        for k in range(2):
            grad_ref[pl.ds(k * half, half), :] += row_home[0, k] + row_home[1, k]
        for copy in scatter:
            copy.wait_send()

    for copy in home:
        copy.wait_send()
    net.finish()


def local(cooc, tile_list, marginal, embed, accum):
    share, width = embed.shape
    half = share // 2
    items = 8 * share
    f32, bf16 = jnp.float32, jnp.bfloat16
    hbm = pl.BlockSpec(memory_space=pl.ANY)
    vmem = pl.BlockSpec(memory_space=pltpu.VMEM)
    smem = pl.BlockSpec(memory_space=pltpu.SMEM)
    summed = pl.pallas_call(
        kernel,
        out_shape=jax.ShapeDtypeStruct((share, width), f32),
        in_specs=[hbm, vmem, smem, hbm],
        out_specs=vmem,
        scratch_shapes=[
            pltpu.VMEM((2, 4, share + PAD, width), f32),
            pltpu.VMEM((2, 2, 4, half + PAD, width), f32),
            pltpu.VMEM((2, half + PAD, width), f32),
            pltpu.VMEM((items, items), jnp.int32),
            pltpu.VMEM((items, width), bf16),
            pltpu.VMEM((items, width), bf16),
            pltpu.VMEM((8, width, share), bf16),
            pltpu.VMEM((8, width, share), bf16),
            pltpu.VMEM((items, width), bf16),
            pltpu.VMEM((items, width), bf16),
            pltpu.VMEM((items, 128), f32),
            pltpu.VMEM((8, PAD, share), f32),
            pltpu.VMEM((2, 2 * share, 2 * share), f32),
            pltpu.VMEM((2, 2, 4, half, width), f32),
            pltpu.VMEM((2, 4, width, share), f32),
            pltpu.VMEM((2, 4, half, width), f32),
            pltpu.VMEM((2, 3, half, width), f32),
            pltpu.VMEM((2, 2, half, width), f32),
            pltpu.VMEM((2, 3, width, share), f32),
            pltpu.VMEM((width, share), f32),
            pltpu.VMEM((8, 8, 128), f32),
            pltpu.VMEM((4, 8, 128), f32),
            pltpu.VMEM((4, 8, 128), f32),
            pltpu.SemaphoreType.DMA((N_SEND,)),
            pltpu.SemaphoreType.DMA((N_RECV,)),
            pltpu.SemaphoreType.DMA((9,)),
        ],
        compiler_params=pltpu.CompilerParams(
            collective_id=0, has_side_effects=True, vmem_limit_bytes=56 * 2**20
        ),
        cost_estimate=pl.CostEstimate(
            flops=18 * items * items * width, bytes_accessed=4 * items * items, transcendentals=0
        ),
    )(embed, marginal.reshape(1, share), tile_list.reshape(1, 4), cooc)
    gradients = summed / (items // 2)
    new_accum = accum + gradients * gradients
    new_embed = embed - LEARN_RATE * gradients / jnp.sqrt(new_accum)
    return (new_embed, new_accum)


def solution(mesh):
    placed = (
        P("row", "col"),
        P("row", "col", None),
        P(("col", "row")),
        P(("col", "row"), None),
        P(("col", "row"), None),
    )
    return jax.shard_map(
        local,
        mesh=mesh,
        in_specs=placed,
        out_specs=(P(("col", "row"), None), P(("col", "row"), None)),
        check_vma=False,
    )
```

time: 558 us -> 100 us (0.18)
  the two profiles are of different devices: /device:TPU:0 before, /device:TPU:26 now
where the time goes in v2:
time: 100 us; the launch traced here: 98.8 us
  Pallas kernels  96.4 us (96%)
  other arithmetic  1.8 us (2%)
    pallas_call x1, Pallas kernels, local(): pl.pallas_call(kernel, out_shape=jax.ShapeDtypeStruct((share, width), f32...  96.4 us

profile of v2, /device:TPU:26, one launch (start us, length us, event | category | flops | bytes accessed | tf_op | source)
XLA Modules:
  0.0 98.8 jit_solution(563267872845187465)
XLA Ops:
  0.6 0.0 copy-start
  0.6 0.0 copy-start.1
  0.7 96.4 %shard_map.68 = f32[256,256]{1,0:T(8,128)} custom-call(f32[256,256]{1,0:T(8,128)} %embed_hbm.1, s32[1,256]{1,0:T(1,128)} %bitcast.2, s32[1,4]{1,0:T(1,128)} %bitcast.3, s32[2048,2048]{1,0:T(8,128)} %cooc_hbm.1), custom_call_target="tpu_custom_call" | custom-call | flops 19327352832 | bytes 16777216 | tf_op jit(solution)/shard_map/pallas_call | solution.py:463
  97.0 0.0 copy-done
  97.0 0.0 copy-done.1
  97.0 1.8 %multiply_subtract_fusion = (f32[256,256]{1,0:T(8,128)}, f32[256,256]{1,0:T(8,128)}) fusion(f32[256,256]{1,0:T(8,128)S(1)} %copy-done, f32[256,256]{1,0:T(8,128)} %shard_map.68, f32[256,256]{1,0:T(8,128)S(1)} %copy-done.1), kind=kLoop, calls=%fused_computation | loop fusion | flops 393216 | bytes 1310720 | tf_op jit(solution)/shard_map/sub | solution.py:505
Async XLA Ops:
  0.6 96.4 %copy-start = (f32[256,256]{1,0:T(8,128)S(1)}, f32[256,256]{1,0:T(8,128)}, u32[]{:S(2)}) copy-start(f32[256,256]{1,0:T(8,128)} %embed_hbm.1) | copy-start | bytes 786436
  0.6 96.4 %copy-start.1 = (f32[256,256]{1,0:T(8,128)S(1)}, f32[256,256]{1,0:T(8,128)}, u32[]{:S(2)}) copy-start(f32[256,256]{1,0:T(8,128)} %param.9) | copy-start | bytes 786436

commit v3 on v2

--- a/solution.py
+++ b/solution.py
@@ -73,6 +73,7 @@
     col_grad,
     sib_in,
     row_in,
+    row_feed,
     row_home,
     col_in,
     col_last,
@@ -115,42 +116,51 @@
     sibling, zl_pair, zh_pair = near[0], near[1], near[3]
     blocks = [lax.rem(zh + zl + s + y // 2, 2) for s in range(2)]
 
-    def piece_y(x_):
-        return lax.rem(zh + 1 + y - x_ + RING, RING)
-
-    source = [(blocks[s] * 4 + piece_y(x), row) for s in range(2)]
-    x_place = lax.rem(x + 1 - y + zl * 2 + q + RING, RING)
+    def piece_y(x_, h):
+        return lax.rem(zh + 1 + 2 * h + y - x_ + RING, RING)
+
+    source = [(blocks[s] * 4 + piece_y(x, q), row) for s in range(2)]
+    relay_self = jnp.logical_and(source[0][0] == row, x * 4 + y == col)
+    x_place = [lax.rem(x + 1 + 2 * k - y + zl * 2 + q + RING, RING) for k in range(2)]
     zl_place = lax.rem(zl + zh + x, 2)
-    targets = [
-        [(col, x_place * 4 + lax.rem(zl_place + s, 2) * 2 + k) for k in range(2)] for s in range(2)
-    ]
+    targets = [(col, x_place[k] * 4 + zl_place * 2 + k) for k in range(2)]
+    relay = [(source[s][0], x * 4 + y) for s in range(2)]
+    relay_y = zl * 2 + q
+    turn = lax.rem(x + 3 + y - relay_y + RING, RING)
+    back_zh, back_h = lax.rem(turn, 2), turn // 2
+    back_zl = lax.rem(zl + zh + back_zh, 2)
+    feeders = [
+        (back_zh * 4 + relay_y, x * 4 + lax.rem(back_zl + s, 2) * 2 + back_h) for s in range(2)
+    ]
+    feeds_self = jnp.logical_and(feeders[0][0] == row, feeders[0][1] == col)
 
     embed_in = pltpu.make_async_copy(
         embed_hbm, col_land.at[zh, y, pl.ds(0, share)], local_sems.at[0]
     )
     embed_in.start()
-    cooc_in = []
-    for p in range(8):
-        copy = pltpu.make_async_copy(
+    cooc_in = [
+        pltpu.make_async_copy(
             cooc_hbm.at[pl.ds(p * share, share)],
             cooc_v.at[pl.ds(p * share, share)],
             local_sems.at[1 + p],
         )
-        copy.start()
-        cooc_in.append(copy)
+        for p in range(8)
+    ]
+
+    def start_cooc():
+        for copy in cooc_in:
+            copy.start()
 
     def signal(other):
         pl.semaphore_signal(barrier, inc=1, device_id=other, device_id_type=MESH)
 
     barrier = pltpu.get_barrier_semaphore()
-    for other in near + near_y + near_x + [source[0]]:
+    for other in near + near_y + near_x + [source[0], feeders[1]]:
         signal(other)
 
-    @pl.when(is_owner)
-    def _():
-        for s in range(2):
-            for other in targets[s]:
-                signal(other)
+    @pl.when(jnp.logical_not(feeds_self))
+    def _():
+        signal(feeders[0])
 
     marg = marg_ref[...].astype(jnp.float32)
     logs = jnp.log(marg)
@@ -163,7 +173,7 @@
             jnp.concatenate([logs[:, h * half : (h + 1) * half]] * 2, axis=1), (PAD, width)
         )
 
-    pl.semaphore_wait(barrier, 15 + jnp.where(is_owner, 2, 0))
+    pl.semaphore_wait(barrier, 14 + jnp.where(relay_self, 0, 1) + jnp.where(is_owner, 2, 0))
 
     net = Copies(send_sems, recv_sems)
 
@@ -199,17 +209,23 @@
     scatter = [
         pltpu.make_async_remote_copy(
             src_ref=row_src.at[k],
-            dst_ref=row_land.at[zl_place, k, x_place],
+            dst_ref=row_land.at[zl_place, k, x_place[k]],
             send_sem=net.send_sem(),
             recv_sem=scatter_recv,
-            device_id=targets[0][k],
+            device_id=targets[k],
             device_id_type=MESH,
         )
         for k in range(2)
     ]
     col_pair = same(col_land.at[zh, y], zh_pair)
     row_pair = same(row_land.at[zl, q, x], zl_pair)
-    col_out = [[same(col_land.at[zhs[s], y], other) for other in by_y] for s in range(2)]
+    col_out = [[same(col_land.at[zhs[s], y], other) for other in by_y[1:]] for s in range(2)]
+    upper, lower = pl.ds(0, half + PAD), pl.ds(half + PAD, half)
+    col_relay = [
+        same(col_land.at[zh, ring(y, -1), upper], by_y[1]),
+        same(col_land.at[zh, ring(y, 1), lower], by_y[2]),
+    ]
+    col_far = same(col_land.at[zh, ring(y, 2)], zh_pair)
     row_out = [[same(row_land.at[zls[s], q, x], other) for other in by_x] for s in range(2)]
     sib_out = [same(row_land.at[zls[s], q], sibling) for s in range(2)]
     sib_parts = [(1, 0, 4), (0, 0, 2), (0, 2, 2)]
@@ -218,45 +234,64 @@
         for s, a, n in sib_parts
     ]
     col_back = [
-        [net.make(col_grad.at[s, o], col_in.at[s, o], by_y[o]) for o in range(3)] for s in range(2)
-    ]
+        [net.make(col_grad.at[0, o], col_in.at[0, o], by_y[o]) for o in range(3)],
+        [net.make(col_grad.at[1, o], col_in.at[1, o], by_y[o]) for o in (1, 2)],
+    ]
+    far_back = net.make(col_grad.at[1, 0], col_in.at[1, 0], zh_pair)
     row_back = [
         [net.make(row_grad.at[q, s, o], row_in.at[s, o], by_x[o]) for o in range(3)]
         for s in range(2)
     ]
     pair_back = net.make(col_grad.at[1, 3], col_last, zh_pair)
-    home_sem = net.recv_sem(4)
-    home = [
+    feed_sem = net.recv_sem(2)
+    feed = [
         pltpu.make_async_remote_copy(
             src_ref=row_grad.at[q, s, 3],
-            dst_ref=row_home.at[s, q],
+            dst_ref=row_feed.at[s],
             send_sem=net.send_sem(),
-            recv_sem=recv_sems.at[home_sem + 2 * s + q],
-            device_id=source[s],
+            recv_sem=recv_sems.at[feed_sem + s],
+            device_id=relay[s],
             device_id_type=MESH,
         )
         for s in range(2)
     ]
-
+    feed_here = pltpu.make_async_copy(
+        row_grad.at[q, 0, 3], row_feed.at[0], recv_sems.at[feed_sem]
+    )
+    home_sem = net.recv_sem(2)
+    home = pltpu.make_async_remote_copy(
+        src_ref=row_feed.at[0],
+        dst_ref=row_home.at[back_h],
+        send_sem=net.send_sem(),
+        recv_sem=recv_sems.at[home_sem + back_h],
+        device_id=device(x_=back_zh),
+        device_id_type=MESH,
+    )
+    ends_here = x == back_zh
+
+    @pl.when(is_owner)
+    def _():
+        start(scatter)
+
+    start(col_out[0])
     stage1 = spread(tot1, near)
-
-    @pl.when(is_owner)
-    def _():
-        start(scatter)
-
-    start([col_pair, col_out[0][1], col_out[0][2], col_out[0][0]])
+    start_cooc()
+    row_grad[...] = jnp.zeros_like(row_grad)
+    col_grad[...] = jnp.zeros_like(col_grad)
     stage1.wait()
     tot2[0] = jnp.sum(tot1[...], axis=0)
     stage2 = spread(tot2, near_x)
     scatter[0].wait_recv()
-    start([row_pair, row_out[0][1], row_out[0][2], row_out[0][0]])
+    start([row_out[0][1], row_out[0][2], row_out[0][0], row_pair, col_pair])
     stage2.wait()
     tot3[0] = jnp.sum(tot2[...], axis=0)
     stage3 = spread(tot3, near_y)
-    row_grad[...] = jnp.zeros_like(row_grad)
-    col_grad[...] = jnp.zeros_like(col_grad)
-    col_pair.wait_recv()
-    start(col_out[1])
+    col_out[0][0].wait_recv()
+    col_relay[0].start()
+    col_out[0][1].wait_recv()
+    col_relay[1].start()
+    arrive(row_out[0])
+    sib_out[0].start()
     row_pair.wait_recv()
     start(row_out[1])
     stage3.wait()
@@ -295,9 +330,10 @@
 
         lax.fori_loop(0, 4, piece, 0)
 
-    arrive(row_out[0])
-    sib_out[0].start()
-    arrive(col_out[0])
+    arrive(col_relay)
+    col_far.start()
+    col_pair.wait_recv()
+    start(col_out[1])
     convert_cols(0)
     for copy in cooc_in:
         copy.wait()
@@ -313,10 +349,11 @@
     def place(s):
         early = s < 8
         late = jnp.maximum(s - 8, 0)
-        rs = jnp.where(early, s // 4, 1 - lax.rem(late // 2, 2))
-        hr = jnp.where(early, lax.rem(s // 2, 2), lax.rem(late, 2))
+        rs = jnp.where(early, s // 4, 1 - late // 4)
+        by_row = jnp.logical_or(early, s >= 12)
+        hr = lax.rem(jnp.where(by_row, s // 2, s), 2)
         cs = jnp.where(early, 0, 1)
-        hc = jnp.where(early, lax.rem(s, 2), late // 4)
+        hc = lax.rem(jnp.where(by_row, s, s // 2), 2)
         return rs, hr, cs, hc
 
     def score(s, slot):
@@ -336,7 +373,13 @@
         zr, zc = jnp.where(rs == 0, blocks[0], blocks[1]), lax.rem(zh + cs, 2)
         first_row, first_col = rs * 4 + hr * 2, cs * 4 + hc * 2
         rows, cols = rows_of(first_row, 2), rows_of(first_col, 2)
-        count_rows = [rows_of(zr * 4 + piece_y(ring(x, k))) for k in (2 + hr, 1 - hr)]
+        count_rows = [
+            pl.ds(
+                pl.multiple_of((zr * 4 + piece_y(ring(x, k), h)) * share + h * half, half), half
+            )
+            for k in (2 + hr, 1 - hr)
+            for h in range(2)
+        ]
         count_cols = [rows_of(zc * 4 + ring(y, k)) for k in (2 + hc, 1 - hc)]
         counts = jnp.concatenate(
             [jnp.concatenate([cooc_v[r, c] for c in count_cols], axis=1) for r in count_rows],
@@ -382,24 +425,40 @@
 
     def before7():
         arrive(col_out[1])
+        col_far.wait_recv()
         convert_cols(1)
 
     def before8():
-        start(col_back[0])
+        start(col_back[0][1:])
 
     def before12():
-        start(col_back[1][:2])
-
-    def before14():
         sib_back[0].start()
 
-    def before15():
-        sib_back[1].start()
+    def before13():
         sib_back[0].wait_recv()
         row_grad[q, 1] += sib_in[1]
         start(row_back[1])
 
-    events = {2: before2, 3: before3, 7: before7, 8: before8, 12: before12, 14: before14, 15: before15}
+    def before14():
+        sib_back[1].start()
+
+    def before15():
+        far_back.start()
+        col_back[1][0].start()
+        sib_back[1].wait_recv()
+        row_grad[q, 0, pl.ds(0, 2)] += sib_in[0, pl.ds(0, 2)]
+        start(row_back[0][:2])
+
+    events = {
+        2: before2,
+        3: before3,
+        7: before7,
+        8: before8,
+        12: before12,
+        13: before13,
+        14: before14,
+        15: before15,
+    }
 
     score(0, 0)
 
@@ -414,41 +473,72 @@
     lax.fori_loop(0, 8, pair, 0)
 
     sib_back[2].start()
-    col_back[1][2].start()
-    sib_back[1].wait_recv()
-    row_grad[q, 0, pl.ds(0, 2)] += sib_in[0, pl.ds(0, 2)]
-    start(row_back[0][:2])
+    col_back[1][1].start()
+    arrive(row_back[1])
+    row_grad[q, 1, 3] += (row_in[1, 0] + row_in[1, 1]) + row_in[1, 2]
+    feed[1].start()
     sib_back[2].wait_recv()
     row_grad[q, 0, pl.ds(2, 2)] += sib_in[0, pl.ds(2, 2)]
     row_back[0][2].start()
+    far_back.wait_recv()
+    col_grad[0, 0] += col_in[1, 0]
+    col_back[0][0].start()
+    arrive(row_back[0])
+    row_grad[q, 0, 3] += (row_in[0, 0] + row_in[0, 1]) + row_in[0, 2]
+
+    @pl.when(relay_self)
+    def _():
+        feed_here.start()
+
+    @pl.when(jnp.logical_not(relay_self))
+    def _():
+        feed[0].start()
+
+    arrive(col_back[1])
+    col_grad[1, 3] += col_in[1, 1] + col_in[1, 2]
+    pair_back.start()
+    for s in range(2):
+        slot = row_feed.at[s]
+        pltpu.make_async_copy(slot, slot, recv_sems.at[feed_sem + s]).wait()
+    row_feed[0] += row_feed[1]
+
+    @pl.when(jnp.logical_not(ends_here))
+    def _():
+        home.start()
+
     arrive(col_back[0])
     col_grad[0, 3] += (col_in[0, 0] + col_in[0, 1]) + col_in[0, 2]
-    arrive(row_back[1])
-    row_grad[q, 1, 3] += (row_in[1, 0] + row_in[1, 1]) + row_in[1, 2]
-
-    home[1].start()
-    arrive(row_back[0])
-    row_grad[q, 0, 3] += (row_in[0, 0] + row_in[0, 1]) + row_in[0, 2]
-    home[0].start()
-    arrive(col_back[1])
-    col_grad[1, 3] += (col_in[1, 0] + col_in[1, 1]) + col_in[1, 2]
-    pair_back.start()
     pair_back.wait_recv()
     grad_ref[...] = (col_grad[0, 3] + col_last[...]).T
 
     @pl.when(is_owner)
     def _():
-        for s in range(2):
-            for k in range(2):
-                slot = row_home.at[s, k]
-                pltpu.make_async_copy(slot, slot, recv_sems.at[home_sem + 2 * s + k]).wait()
         for k in range(2):
-            grad_ref[pl.ds(k * half, half), :] += row_home[0, k] + row_home[1, k]
+            part = pl.ds(k * half, half)
+
+            @pl.when(x_place[k] == x)
+            def _():
+                grad_ref[part, :] += row_feed[0]
+
+            @pl.when(x_place[k] != x)
+            def _():
+                slot = row_home.at[k]
+                pltpu.make_async_copy(slot, slot, recv_sems.at[home_sem + k]).wait()
+                grad_ref[part, :] += row_home[k]
+
         for copy in scatter:
             copy.wait_send()
 
-    for copy in home:
-        copy.wait_send()
+    @pl.when(jnp.logical_not(relay_self))
+    def _():
+        feed[0].wait_send()
+
+    feed[1].wait_send()
+
+    @pl.when(jnp.logical_not(ends_here))
+    def _():
+        home.wait_send()
+
     net.finish()
 
 
@@ -483,7 +573,8 @@
             pltpu.VMEM((2, 4, width, share), f32),
             pltpu.VMEM((2, 4, half, width), f32),
             pltpu.VMEM((2, 3, half, width), f32),
-            pltpu.VMEM((2, 2, half, width), f32),
+            pltpu.VMEM((2, half, width), f32),
+            pltpu.VMEM((2, half, width), f32),
             pltpu.VMEM((2, 3, width, share), f32),
             pltpu.VMEM((width, share), f32),
             pltpu.VMEM((8, 8, 128), f32),

time: 100 us -> 86.3 us (0.86)
  Pallas kernels: 96.4 us -> 83.6 us
    pallas_call x1, Pallas kernels: 96.4 us -> 83.6 us  [local(): pl.pallas_call(kernel, out_shape=jax.ShapeDtypeStruct((share, width), f32...]
where the time goes in v3:
time: 86.3 us; the launch traced here: 86.1 us
  Pallas kernels  83.6 us (97%)
  other arithmetic  1.8 us (2%)
    pallas_call x1, Pallas kernels, local(): pl.pallas_call(kernel, out_shape=jax.ShapeDtypeStruct((share, width), f32...  83.6 us
    sub x1, other arithmetic, local(): new_embed = embed - LEARN_RATE * gradients / jnp.sqrt(new_accum)  1.8 us

profile of v3, /device:TPU:26, one launch (start us, length us, event | category | flops | bytes accessed | tf_op | source)
XLA Modules:
  0.0 86.1 jit_solution(8968589652015641897)
XLA Ops:
  0.6 0.0 copy-start
  0.6 0.0 copy-start.1
  0.7 83.6 %shard_map.68 = f32[256,256]{1,0:T(8,128)} custom-call(f32[256,256]{1,0:T(8,128)} %embed_hbm.1, s32[1,256]{1,0:T(1,128)} %bitcast.2, s32[1,4]{1,0:T(1,128)} %bitcast.3, s32[2048,2048]{1,0:T(8,128)} %cooc_hbm.1), custom_call_target="tpu_custom_call" | custom-call | flops 19327352832 | bytes 16777216 | tf_op jit(solution)/shard_map/pallas_call | solution.py:553
  84.3 0.0 copy-done
  84.3 0.0 copy-done.1
  84.3 1.8 %multiply_subtract_fusion = (f32[256,256]{1,0:T(8,128)}, f32[256,256]{1,0:T(8,128)}) fusion(f32[256,256]{1,0:T(8,128)S(1)} %copy-done, f32[256,256]{1,0:T(8,128)} %shard_map.68, f32[256,256]{1,0:T(8,128)S(1)} %copy-done.1), kind=kLoop, calls=%fused_computation | loop fusion | flops 393216 | bytes 1310720 | tf_op jit(solution)/shard_map/sub | solution.py:596
Async XLA Ops:
  0.6 83.6 %copy-start = (f32[256,256]{1,0:T(8,128)S(1)}, f32[256,256]{1,0:T(8,128)}, u32[]{:S(2)}) copy-start(f32[256,256]{1,0:T(8,128)} %embed_hbm.1) | copy-start | bytes 786436
  0.6 83.6 %copy-start.1 = (f32[256,256]{1,0:T(8,128)S(1)}, f32[256,256]{1,0:T(8,128)}, u32[]{:S(2)}) copy-start(f32[256,256]{1,0:T(8,128)} %param.9) | copy-start | bytes 786436

commit v4 on v3

--- a/solution.py
+++ b/solution.py
@@ -98,7 +98,7 @@
         return lax.rem(position + step + RING, RING)
 
     def offset(o):
-        return jnp.where(o == 0, 2, jnp.where(o == 1, 1, jnp.where(o == 2, 3, 0)))
+        return jnp.where(o == 0, 1, jnp.where(o == 1, 3, jnp.where(o == 2, 2, 0)))
 
     is_owner = col < 8
 
@@ -111,8 +111,8 @@
     ]
     near_y = [device(y_=ring(y, k)) for k in range(1, 4)]
     near_x = [device(x_=ring(x, k)) for k in range(1, 4)]
-    by_y = [near_y[1], near_y[0], near_y[2]]
-    by_x = [near_x[1], near_x[0], near_x[2]]
+    by_y = [near_y[0], near_y[2], near_y[1]]
+    by_x = [near_x[0], near_x[2], near_x[1]]
     sibling, zl_pair, zh_pair = near[0], near[1], near[3]
     blocks = [lax.rem(zh + zl + s + y // 2, 2) for s in range(2)]
 
@@ -147,9 +147,8 @@
         for p in range(8)
     ]
 
-    def start_cooc():
-        for copy in cooc_in:
-            copy.start()
+    for copy in cooc_in:
+        copy.start()
 
     def signal(other):
         pl.semaphore_signal(barrier, inc=1, device_id=other, device_id_type=MESH)
@@ -219,25 +218,26 @@
     ]
     col_pair = same(col_land.at[zh, y], zh_pair)
     row_pair = same(row_land.at[zl, q, x], zl_pair)
-    col_out = [[same(col_land.at[zhs[s], y], other) for other in by_y[1:]] for s in range(2)]
+    col_out = [[same(col_land.at[zhs[s], y], other) for other in by_y[:2]] for s in range(2)]
     upper, lower = pl.ds(0, half + PAD), pl.ds(half + PAD, half)
     col_relay = [
-        same(col_land.at[zh, ring(y, -1), upper], by_y[1]),
-        same(col_land.at[zh, ring(y, 1), lower], by_y[2]),
+        same(col_land.at[zh, ring(y, -1), upper], by_y[0]),
+        same(col_land.at[zh, ring(y, 1), lower], by_y[1]),
     ]
     col_far = same(col_land.at[zh, ring(y, 2)], zh_pair)
     row_out = [[same(row_land.at[zls[s], q, x], other) for other in by_x] for s in range(2)]
-    sib_out = [same(row_land.at[zls[s], q], sibling) for s in range(2)]
-    sib_parts = [(1, 0, 4), (0, 0, 2), (0, 2, 2)]
+    sib_pieces = [same(row_land.at[zl, q, ring(x, step)], sibling) for step in (1, 3, 2, 0)]
+    sib_block = same(row_land.at[1 - zl, q], sibling)
+    sib_parts = [(0, 0, 4), (1, 0, 2), (1, 2, 2)]
     sib_back = [
         net.make(row_grad.at[1 - q, s, pl.ds(a, n)], sib_in.at[s, pl.ds(a, n)], sibling)
         for s, a, n in sib_parts
     ]
     col_back = [
         [net.make(col_grad.at[0, o], col_in.at[0, o], by_y[o]) for o in range(3)],
-        [net.make(col_grad.at[1, o], col_in.at[1, o], by_y[o]) for o in (1, 2)],
-    ]
-    far_back = net.make(col_grad.at[1, 0], col_in.at[1, 0], zh_pair)
+        [net.make(col_grad.at[1, o], col_in.at[1, o], by_y[o]) for o in range(2)],
+    ]
+    far_back = net.make(col_grad.at[1, 2], col_in.at[1, 2], zh_pair)
     row_back = [
         [net.make(row_grad.at[q, s, o], row_in.at[s, o], by_x[o]) for o in range(3)]
         for s in range(2)
@@ -275,14 +275,13 @@
 
     start(col_out[0])
     stage1 = spread(tot1, near)
-    start_cooc()
     row_grad[...] = jnp.zeros_like(row_grad)
     col_grad[...] = jnp.zeros_like(col_grad)
     stage1.wait()
     tot2[0] = jnp.sum(tot1[...], axis=0)
     stage2 = spread(tot2, near_x)
     scatter[0].wait_recv()
-    start([row_out[0][1], row_out[0][2], row_out[0][0], row_pair, col_pair])
+    start([*row_out[0][:2], sib_pieces[3], row_out[0][2], row_pair, col_pair])
     stage2.wait()
     tot3[0] = jnp.sum(tot2[...], axis=0)
     stage3 = spread(tot3, near_y)
@@ -290,17 +289,16 @@
     col_relay[0].start()
     col_out[0][1].wait_recv()
     col_relay[1].start()
-    arrive(row_out[0])
-    sib_out[0].start()
-    row_pair.wait_recv()
-    start(row_out[1])
+    for k in range(2):
+        row_out[0][k].wait_recv()
+        sib_pieces[1 - k].start()
     stage3.wait()
     log_total = jnp.log(jnp.sum(tot3[...], axis=0))[:1, :1]
 
     def rows_of(index, count=1):
         return pl.ds(pl.multiple_of(index * share, share), count * share)
 
-    def convert_cols(s):
+    def convert_cols(s, first, last):
         def piece(o, carry):
             at = ring(y, offset(o))
             index = s * 4 + o
@@ -309,9 +307,9 @@
             col_log[index] = col_land[zhs[s], at, pl.ds(share, PAD), :] - log_total
             return carry
 
-        lax.fori_loop(0, 4, piece, 0)
-
-    def convert_rows(s):
+        lax.fori_loop(first, last, piece, 0)
+
+    def convert_rows(s, first, last):
         def piece(o, carry):
             at = ring(x, offset(o))
             index = s * 4 + o
@@ -328,17 +326,21 @@
                 ] = jnp.broadcast_to(line, (128, half)).T
             return carry
 
-        lax.fori_loop(0, 4, piece, 0)
+        lax.fori_loop(first, last, piece, 0)
 
     arrive(col_relay)
     col_far.start()
     col_pair.wait_recv()
     start(col_out[1])
-    convert_cols(0)
+    convert_cols(0, 0, 4)
+    arrive(sib_pieces[:2])
+    convert_rows(0, 0, 2)
+    row_out[0][2].wait_recv()
+    sib_pieces[2].start()
+    row_pair.wait_recv()
+    start(row_out[1])
     for copy in cooc_in:
         copy.wait()
-    sib_out[0].wait_recv()
-    convert_rows(0)
 
     entries = [tiles_ref[0, k] for k in range(4)]
 
@@ -347,12 +349,10 @@
         return (on[0] + on[1]) + (on[2] + on[3])
 
     def place(s):
-        early = s < 8
-        late = jnp.maximum(s - 8, 0)
-        rs = jnp.where(early, s // 4, 1 - late // 4)
-        by_row = jnp.logical_or(early, s >= 12)
+        rs = s // 8
+        cs = jnp.where(jnp.logical_and(s >= 4, s < 12), 1, 0)
+        by_row = jnp.logical_or(s < 8, s >= 12)
         hr = lax.rem(jnp.where(by_row, s // 2, s), 2)
-        cs = jnp.where(early, 0, 1)
         hc = lax.rem(jnp.where(by_row, s, s // 2), 2)
         return rs, hr, cs, hc
 
@@ -377,10 +377,10 @@
             pl.ds(
                 pl.multiple_of((zr * 4 + piece_y(ring(x, k), h)) * share + h * half, half), half
             )
-            for k in (2 + hr, 1 - hr)
+            for k in (1 + hr, 3 - 3 * hr)
             for h in range(2)
         ]
-        count_cols = [rows_of(zc * 4 + ring(y, k)) for k in (2 + hc, 1 - hc)]
+        count_cols = [rows_of(zc * 4 + ring(y, k)) for k in (1 + hc, 3 - 3 * hc)]
         counts = jnp.concatenate(
             [jnp.concatenate([cooc_v[r, c] for c in count_cols], axis=1) for r in count_rows],
             axis=0,
@@ -391,7 +391,7 @@
         counts_f = jnp.maximum(counts.astype(jnp.float32), 1.0)
         slopes = listed(zr * 2 + zc) * jnp.where(
             counts > 0,
-            (0.1 + 0.25 * jnp.sqrt(counts_f)) * (centred - jnp.log(counts_f)),
+            (0.1 + 0.25 * (counts_f * lax.rsqrt(counts_f))) * (centred - jnp.log(counts_f)),
             1.0 / (1.0 + jnp.exp(-centred)),
         )
         sh, sl = split(slopes)
@@ -415,47 +415,72 @@
         for k in range(2):
             col_grad[cs, hc * 2 + k] += to_cols[:, k * share : (k + 1) * share]
 
-    def before2():
+    def before1():
+        arrive(sib_pieces[2:])
+        convert_rows(0, 2, 4)
+
+    def before3():
+        arrive(col_out[1])
+        convert_cols(1, 0, 2)
+
+    def before4():
+        col_far.wait_recv()
+        convert_cols(1, 2, 4)
+
+    def before5():
         arrive(row_out[1])
-        sib_out[1].start()
-
-    def before3():
-        sib_out[1].wait_recv()
-        convert_rows(1)
+        sib_block.start()
 
     def before7():
-        arrive(col_out[1])
-        col_far.wait_recv()
-        convert_cols(1)
+        sib_block.wait_recv()
+        convert_rows(1, 0, 4)
 
     def before8():
-        start(col_back[0][1:])
+        sib_back[0].start()
+
+    def before9():
+        sib_back[0].wait_recv()
+        row_grad[q, 0] += sib_in[0]
+        start(row_back[0])
+
+    def before10():
+        start(col_back[1])
 
     def before12():
-        sib_back[0].start()
-
-    def before13():
-        sib_back[0].wait_recv()
-        row_grad[q, 1] += sib_in[1]
-        start(row_back[1])
+        far_back.start()
 
     def before14():
         sib_back[1].start()
+        arrive(row_back[0])
+        row_grad[q, 0, 3] += (row_in[0, 0] + row_in[0, 1]) + row_in[0, 2]
+
+        @pl.when(relay_self)
+        def _():
+            feed_here.start()
+
+        @pl.when(jnp.logical_not(relay_self))
+        def _():
+            feed[0].start()
 
     def before15():
-        far_back.start()
-        col_back[1][0].start()
+        start(col_back[0][:2])
         sib_back[1].wait_recv()
-        row_grad[q, 0, pl.ds(0, 2)] += sib_in[0, pl.ds(0, 2)]
-        start(row_back[0][:2])
+        row_grad[q, 1, pl.ds(0, 2)] += sib_in[1, pl.ds(0, 2)]
+        start(row_back[1][:2])
+        arrive(col_back[1])
+        col_grad[1, 3] += col_in[1, 0] + col_in[1, 1]
+        pair_back.start()
 
     events = {
-        2: before2,
+        1: before1,
         3: before3,
+        4: before4,
+        5: before5,
         7: before7,
         8: before8,
+        9: before9,
+        10: before10,
         12: before12,
-        13: before13,
         14: before14,
         15: before15,
     }
@@ -473,30 +498,15 @@
     lax.fori_loop(0, 8, pair, 0)
 
     sib_back[2].start()
-    col_back[1][1].start()
+    far_back.wait_recv()
+    col_grad[0, 2] += col_in[1, 2]
+    col_back[0][2].start()
+    sib_back[2].wait_recv()
+    row_grad[q, 1, pl.ds(2, 2)] += sib_in[1, pl.ds(2, 2)]
+    row_back[1][2].start()
     arrive(row_back[1])
     row_grad[q, 1, 3] += (row_in[1, 0] + row_in[1, 1]) + row_in[1, 2]
     feed[1].start()
-    sib_back[2].wait_recv()
-    row_grad[q, 0, pl.ds(2, 2)] += sib_in[0, pl.ds(2, 2)]
-    row_back[0][2].start()
-    far_back.wait_recv()
-    col_grad[0, 0] += col_in[1, 0]
-    col_back[0][0].start()
-    arrive(row_back[0])
-    row_grad[q, 0, 3] += (row_in[0, 0] + row_in[0, 1]) + row_in[0, 2]
-
-    @pl.when(relay_self)
-    def _():
-        feed_here.start()
-
-    @pl.when(jnp.logical_not(relay_self))
-    def _():
-        feed[0].start()
-
-    arrive(col_back[1])
-    col_grad[1, 3] += col_in[1, 1] + col_in[1, 2]
-    pair_back.start()
     for s in range(2):
         slot = row_feed.at[s]
         pltpu.make_async_copy(slot, slot, recv_sems.at[feed_sem + s]).wait()

time: 86.3 us -> 81.4 us (0.943)
  Pallas kernels: 83.6 us -> 78.2 us
    pallas_call x1, Pallas kernels: 83.6 us -> 78.2 us  [local(): pl.pallas_call(kernel, out_shape=jax.ShapeDtypeStruct((share, width), f32...]
where the time goes in v4:
time: 81.4 us; the launch traced here: 80.7 us
  Pallas kernels  78.2 us (96%)
  other arithmetic  1.8 us (2%)
    pallas_call x1, Pallas kernels, local(): pl.pallas_call(kernel, out_shape=jax.ShapeDtypeStruct((share, width), f32...  78.2 us
    sub x1, other arithmetic, local(): new_embed = embed - LEARN_RATE * gradients / jnp.sqrt(new_accum)  1.8 us

profile of v4, /device:TPU:26, one launch (start us, length us, event | category | flops | bytes accessed | tf_op | source)
XLA Modules:
  0.0 80.7 jit_solution(16702933399417616847)
XLA Ops:
  0.6 0.0 copy-start
  0.6 0.0 copy-start.1
  0.7 78.2 %shard_map.68 = f32[256,256]{1,0:T(8,128)} custom-call(f32[256,256]{1,0:T(8,128)} %embed_hbm.1, s32[1,256]{1,0:T(1,128)} %bitcast.2, s32[1,4]{1,0:T(1,128)} %bitcast.3, s32[2048,2048]{1,0:T(8,128)} %cooc_hbm.1), custom_call_target="tpu_custom_call" | custom-call | flops 19327352832 | bytes 16777216 | tf_op jit(solution)/shard_map/pallas_call | solution.py:563
  78.8 0.0 copy-done
  78.8 0.0 copy-done.1
  78.9 1.8 %multiply_subtract_fusion = (f32[256,256]{1,0:T(8,128)}, f32[256,256]{1,0:T(8,128)}) fusion(f32[256,256]{1,0:T(8,128)S(1)} %copy-done, f32[256,256]{1,0:T(8,128)} %shard_map.68, f32[256,256]{1,0:T(8,128)S(1)} %copy-done.1), kind=kLoop, calls=%fused_computation | loop fusion | flops 393216 | bytes 1310720 | tf_op jit(solution)/shard_map/sub | solution.py:606
Async XLA Ops:
  0.6 78.2 %copy-start = (f32[256,256]{1,0:T(8,128)S(1)}, f32[256,256]{1,0:T(8,128)}, u32[]{:S(2)}) copy-start(f32[256,256]{1,0:T(8,128)} %embed_hbm.1) | copy-start | bytes 786436
  0.6 78.2 %copy-start.1 = (f32[256,256]{1,0:T(8,128)S(1)}, f32[256,256]{1,0:T(8,128)}, u32[]{:S(2)}) copy-start(f32[256,256]{1,0:T(8,128)} %param.9) | copy-start | bytes 786436

commit v5 on v4

--- a/solution.py
+++ b/solution.py
@@ -52,8 +52,8 @@
 
 def kernel(
     embed_hbm,
-    marg_ref,
-    tiles_ref,
+    marg_hbm,
+    tiles_hbm,
     cooc_hbm,
     grad_ref,
     col_land,
@@ -77,6 +77,8 @@
     row_home,
     col_in,
     col_last,
+    marg_ref,
+    tiles_ref,
     tot1,
     tot2,
     tot3,
@@ -134,10 +136,25 @@
     ]
     feeds_self = jnp.logical_and(feeders[0][0] == row, feeders[0][1] == col)
 
+    def signal(other):
+        pl.semaphore_signal(barrier, inc=1, device_id=other, device_id_type=MESH)
+
+    barrier = pltpu.get_barrier_semaphore()
+    for other in near + near_y + near_x + [source[0], feeders[1]]:
+        signal(other)
+
+    @pl.when(jnp.logical_not(feeds_self))
+    def _():
+        signal(feeders[0])
+
     embed_in = pltpu.make_async_copy(
         embed_hbm, col_land.at[zh, y, pl.ds(0, share)], local_sems.at[0]
     )
     embed_in.start()
+    marg_in = pltpu.make_async_copy(marg_hbm, marg_ref, local_sems.at[9])
+    marg_in.start()
+    tiles_in = pltpu.make_async_copy(tiles_hbm, tiles_ref, local_sems.at[10])
+    tiles_in.start()
     cooc_in = [
         pltpu.make_async_copy(
             cooc_hbm.at[pl.ds(p * share, share)],
@@ -150,17 +167,7 @@
     for copy in cooc_in:
         copy.start()
 
-    def signal(other):
-        pl.semaphore_signal(barrier, inc=1, device_id=other, device_id_type=MESH)
-
-    barrier = pltpu.get_barrier_semaphore()
-    for other in near + near_y + near_x + [source[0], feeders[1]]:
-        signal(other)
-
-    @pl.when(jnp.logical_not(feeds_self))
-    def _():
-        signal(feeders[0])
-
+    marg_in.wait()
     marg = marg_ref[...].astype(jnp.float32)
     logs = jnp.log(marg)
     tot1[0] = jnp.broadcast_to(jnp.sum(marg, axis=1, keepdims=True), tot1.shape[1:])
@@ -281,7 +288,7 @@
     tot2[0] = jnp.sum(tot1[...], axis=0)
     stage2 = spread(tot2, near_x)
     scatter[0].wait_recv()
-    start([*row_out[0][:2], sib_pieces[3], row_out[0][2], row_pair, col_pair])
+    start([*row_out[0][:2], sib_pieces[3], row_out[0][2], col_pair, row_pair])
     stage2.wait()
     tot3[0] = jnp.sum(tot2[...], axis=0)
     stage3 = spread(tot3, near_y)
@@ -328,10 +335,10 @@
 
         lax.fori_loop(first, last, piece, 0)
 
+    col_pair.wait_recv()
+    start(col_out[1])
     arrive(col_relay)
     col_far.start()
-    col_pair.wait_recv()
-    start(col_out[1])
     convert_cols(0, 0, 4)
     arrive(sib_pieces[:2])
     convert_rows(0, 0, 2)
@@ -342,6 +349,7 @@
     for copy in cooc_in:
         copy.wait()
 
+    tiles_in.wait()
     entries = [tiles_ref[0, k] for k in range(4)]
 
     def listed(t):
@@ -351,7 +359,7 @@
     def place(s):
         rs = s // 8
         cs = jnp.where(jnp.logical_and(s >= 4, s < 12), 1, 0)
-        by_row = jnp.logical_or(s < 8, s >= 12)
+        by_row = jnp.logical_or(s < 4, s >= 12)
         hr = lax.rem(jnp.where(by_row, s // 2, s), 2)
         hc = lax.rem(jnp.where(by_row, s, s // 2), 2)
         return rs, hr, cs, hc
@@ -423,13 +431,11 @@
         arrive(col_out[1])
         convert_cols(1, 0, 2)
 
-    def before4():
-        col_far.wait_recv()
-        convert_cols(1, 2, 4)
-
     def before5():
         arrive(row_out[1])
         sib_block.start()
+        col_far.wait_recv()
+        convert_cols(1, 2, 4)
 
     def before7():
         sib_block.wait_recv()
@@ -474,7 +480,6 @@
     events = {
         1: before1,
         3: before3,
-        4: before4,
         5: before5,
         7: before7,
         8: before8,
@@ -559,11 +564,10 @@
     f32, bf16 = jnp.float32, jnp.bfloat16
     hbm = pl.BlockSpec(memory_space=pl.ANY)
     vmem = pl.BlockSpec(memory_space=pltpu.VMEM)
-    smem = pl.BlockSpec(memory_space=pltpu.SMEM)
     summed = pl.pallas_call(
         kernel,
         out_shape=jax.ShapeDtypeStruct((share, width), f32),
-        in_specs=[hbm, vmem, smem, hbm],
+        in_specs=[hbm, hbm, hbm, hbm],
         out_specs=vmem,
         scratch_shapes=[
             pltpu.VMEM((2, 4, share + PAD, width), f32),
@@ -587,12 +591,14 @@
             pltpu.VMEM((2, half, width), f32),
             pltpu.VMEM((2, 3, width, share), f32),
             pltpu.VMEM((width, share), f32),
+            pltpu.VMEM((1, share), jnp.int32),
+            pltpu.SMEM((1, 4), jnp.int32),
             pltpu.VMEM((8, 8, 128), f32),
             pltpu.VMEM((4, 8, 128), f32),
             pltpu.VMEM((4, 8, 128), f32),
             pltpu.SemaphoreType.DMA((N_SEND,)),
             pltpu.SemaphoreType.DMA((N_RECV,)),
-            pltpu.SemaphoreType.DMA((9,)),
+            pltpu.SemaphoreType.DMA((11,)),
         ],
         compiler_params=pltpu.CompilerParams(
             collective_id=0, has_side_effects=True, vmem_limit_bytes=56 * 2**20

time: 81.4 us -> 80 us (0.983)
  no operation moved by 1% of the time
where the time goes in v5:
time: 80 us; the launch traced here: 79.9 us
  Pallas kernels  77.4 us (97%)
  other arithmetic  1.8 us (2%)
    pallas_call x1, Pallas kernels, local(): pl.pallas_call(kernel, out_shape=jax.ShapeDtypeStruct((share, width), f32...  77.4 us
    sub x1, other arithmetic, local(): new_embed = embed - LEARN_RATE * gradients / jnp.sqrt(new_accum)  1.8 us

profile of v5, /device:TPU:26, one launch (start us, length us, event | category | flops | bytes accessed | tf_op | source)
XLA Modules:
  0.0 79.9 jit_solution(11579133971007837408)
XLA Ops:
  0.6 0.0 copy-start
  0.6 0.0 copy-start.1
  0.7 77.4 %shard_map.68 = f32[256,256]{1,0:T(8,128)} custom-call(f32[256,256]{1,0:T(8,128)} %embed_hbm.1, s32[1,256]{1,0:T(1,128)} %bitcast.2, s32[1,4]{1,0:T(1,128)} %bitcast.3, s32[2048,2048]{1,0:T(8,128)} %cooc_hbm.1), custom_call_target="tpu_custom_call" | custom-call | flops 19327352832 | bytes 16777216 | tf_op jit(solution)/shard_map/pallas_call | solution.py:567
  78.1 0.0 copy-done
  78.1 0.0 copy-done.1
  78.1 1.8 %multiply_subtract_fusion = (f32[256,256]{1,0:T(8,128)}, f32[256,256]{1,0:T(8,128)}) fusion(f32[256,256]{1,0:T(8,128)S(1)} %copy-done, f32[256,256]{1,0:T(8,128)} %shard_map.68, f32[256,256]{1,0:T(8,128)S(1)} %copy-done.1), kind=kLoop, calls=%fused_computation | loop fusion | flops 393216 | bytes 1310720 | tf_op jit(solution)/shard_map/sub | solution.py:612
Async XLA Ops:
  0.6 77.4 %copy-start = (f32[256,256]{1,0:T(8,128)S(1)}, f32[256,256]{1,0:T(8,128)}, u32[]{:S(2)}) copy-start(f32[256,256]{1,0:T(8,128)} %embed_hbm.1) | copy-start | bytes 786436
  0.6 77.4 %copy-start.1 = (f32[256,256]{1,0:T(8,128)S(1)}, f32[256,256]{1,0:T(8,128)}, u32[]{:S(2)}) copy-start(f32[256,256]{1,0:T(8,128)} %param.9) | copy-start | bytes 786436

commit v6 on v5

--- a/solution.py
+++ b/solution.py
@@ -375,8 +375,9 @@
             preferred_element_type=jnp.float32,
         )
 
-    def work(s, slot):
-        score(jnp.minimum(s + 1, 15), 1 - slot)
+    def work(s, slot, ahead=True):
+        if ahead:
+            score(s + 1, 1 - slot)
         rs, hr, cs, hc = place(s)
         zr, zc = jnp.where(rs == 0, blocks[0], blocks[1]), lax.rem(zh + cs, 2)
         first_row, first_col = rs * 4 + hr * 2, cs * 4 + hc * 2
@@ -486,8 +487,6 @@
         9: before9,
         10: before10,
         12: before12,
-        14: before14,
-        15: before15,
     }
 
     score(0, 0)
@@ -500,15 +499,19 @@
             work(2 * i + u, u)
         return carry
 
-    lax.fori_loop(0, 8, pair, 0)
+    lax.fori_loop(0, 7, pair, 0)
+    before14()
+    work(14, 0)
+    before15()
+    work(15, 1, ahead=False)
 
     sib_back[2].start()
+    sib_back[2].wait_recv()
+    row_grad[q, 1, pl.ds(2, 2)] += sib_in[1, pl.ds(2, 2)]
+    row_back[1][2].start()
     far_back.wait_recv()
     col_grad[0, 2] += col_in[1, 2]
     col_back[0][2].start()
-    sib_back[2].wait_recv()
-    row_grad[q, 1, pl.ds(2, 2)] += sib_in[1, pl.ds(2, 2)]
-    row_back[1][2].start()
     arrive(row_back[1])
     row_grad[q, 1, 3] += (row_in[1, 0] + row_in[1, 1]) + row_in[1, 2]
     feed[1].start()

time: 80 us -> 79.6 us (level)
  no operation moved by 1% of the time
where the time goes in v6:
time: 79.6 us; the launch traced here: 79.5 us
  Pallas kernels  77 us (97%)
  other arithmetic  1.8 us (2%)
    pallas_call x1, Pallas kernels, local(): pl.pallas_call(kernel, out_shape=jax.ShapeDtypeStruct((share, width), f32...  77 us
    sub x1, other arithmetic, local(): new_embed = embed - LEARN_RATE * gradients / jnp.sqrt(new_accum)  1.8 us

profile of v6, /device:TPU:26, one launch (start us, length us, event | category | flops | bytes accessed | tf_op | source)
XLA Modules:
  0.0 79.5 jit_solution(6522210293045307666)
XLA Ops:
  0.6 0.0 copy-start
  0.6 0.0 copy-start.1
  0.7 77.0 %shard_map.68 = f32[256,256]{1,0:T(8,128)} custom-call(f32[256,256]{1,0:T(8,128)} %embed_hbm.1, s32[1,256]{1,0:T(1,128)} %bitcast.2, s32[1,4]{1,0:T(1,128)} %bitcast.3, s32[2048,2048]{1,0:T(8,128)} %cooc_hbm.1), custom_call_target="tpu_custom_call" | custom-call | flops 19327352832 | bytes 16777216 | tf_op jit(solution)/shard_map/pallas_call | solution.py:570
  77.7 0.0 copy-done
  77.7 0.0 copy-done.1
  77.7 1.8 %multiply_subtract_fusion = (f32[256,256]{1,0:T(8,128)}, f32[256,256]{1,0:T(8,128)}) fusion(f32[256,256]{1,0:T(8,128)S(1)} %copy-done, f32[256,256]{1,0:T(8,128)} %shard_map.68, f32[256,256]{1,0:T(8,128)S(1)} %copy-done.1), kind=kLoop, calls=%fused_computation | loop fusion | flops 393216 | bytes 1310720 | tf_op jit(solution)/shard_map/sub | solution.py:615
Async XLA Ops:
  0.6 77.0 %copy-start = (f32[256,256]{1,0:T(8,128)S(1)}, f32[256,256]{1,0:T(8,128)}, u32[]{:S(2)}) copy-start(f32[256,256]{1,0:T(8,128)} %embed_hbm.1) | copy-start | bytes 786436
  0.6 77.0 %copy-start.1 = (f32[256,256]{1,0:T(8,128)S(1)}, f32[256,256]{1,0:T(8,128)}, u32[]{:S(2)}) copy-start(f32[256,256]{1,0:T(8,128)} %param.9) | copy-start | bytes 786436
